TPU v7x, 128 devices: a whole 4x4x4 slice. The times are simulated.
128 devices in a mesh: space: 32 (over y, x, core), tm: 4 (over z).
Axes of the slice: x: 4, y: 4, z: 4, core: 2. Of those that a mesh axis runs over, the one named last changes fastest.
Arguments:
- field: bfloat16 [192, 1440, 1024], P('space', None, 'tm'), may hold values from -72 to 72
- sketch: bfloat16 [192, 1440, 512], P('space'), may hold values from -0.01171875 to 0.01171875
Outputs:
- basis: float32 [1024, 512], P(('tm', 'space'))
- r_factor: float32 [512, 512], replicated
All inputs are finite; a program needn't handle non-finite values.
Results may differ from a plain program's by a relative error of at most 0.02.
Values may be sent and summed in bfloat16 or wider, within the bound.
A program may use at most 256 MiB of HBM per device.

v0:
```python
import math

import jax
import jax.numpy as jnp
from jax import lax
from jax.sharding import PartitionSpec as P

HALO = 120


low_cutoff = 1.0 / 240.0
high_cutoff = 0.4
smooth_taps = (1.0 / 16.0, 4.0 / 16.0, 6.0 / 16.0, 4.0 / 16.0, 1.0 / 16.0)


def padded_2(x, sides, width):
    for axis, dim in sides:
        devices, length = (lax.axis_size(axis), x.shape[dim])
        up = [(i, (i + 1) % devices) for i in range(devices - 1)]
        down = [(j, i) for i, j in up]
        last = lax.slice_in_dim(x, length - width, length, axis=dim)
        leading = lax.slice_in_dim(x, 0, width, axis=dim)
        before = lax.ppermute(last, axis, up)
        after = lax.ppermute(leading, axis, down)
        x = jnp.concatenate([before, x, after], axis=dim)
    return x


def band_matrix(span):
    rows_idx = jnp.arange(span + 2 * HALO, dtype=jnp.float32)
    cols_idx = jnp.arange(span, dtype=jnp.float32)
    offset = rows_idx[:, None] - cols_idx[None, :] - HALO
    value = 2.0 * high_cutoff * jnp.sinc(2.0 * high_cutoff * offset) - 2.0 * low_cutoff * jnp.sinc(
        2.0 * low_cutoff * offset
    )
    value = value * jnp.sinc(offset / (HALO + 1.0))
    inside = jnp.abs(offset) <= HALO
    return jnp.where(inside, value, jnp.zeros_like(value)).astype(jnp.bfloat16)


def smooth_rows(padded):
    count = padded.shape[0] - 4
    across = smooth_taps[0] * padded[0:count].astype(jnp.float32)
    for shift in range(1, 5):
        across = across + smooth_taps[shift] * padded[shift : shift + count].astype(jnp.float32)
    total = smooth_taps[2] * across
    for shift in (0, 1, 3, 4):
        total = total + smooth_taps[shift] * jnp.roll(across, 2 - shift, axis=1)
    return total.astype(jnp.bfloat16)


def body(field, sketch):
    block_hours = field.shape[2]
    widened = padded_2(field, (("tm", 2),), HALO)
    taller = padded_2(widened, (("space", 0),), 2)
    smooth = smooth_rows(taller)
    flat = smooth.reshape(-1, block_hours + 2 * HALO)
    band = band_matrix(block_hours)
    filtered = jnp.dot(flat, band, preferred_element_type=jnp.float32).astype(jnp.bfloat16)
    wide = filtered.astype(jnp.float32)
    energy = lax.psum(jnp.sum(wide * wide, axis=1), "tm")
    all_hours = block_hours * lax.axis_size("tm")
    inverse = lax.rsqrt(energy / all_hours + 1e-06)
    standard = (wide * inverse[:, None]).astype(jnp.bfloat16)
    omega = sketch.reshape(-1, sketch.shape[2])
    columns = lax.slice_in_dim(
        standard, 0, lax.axis_size("space") * (block_hours // lax.axis_size("space")), axis=1
    )
    own_rows = lax.psum_scatter(
        lax.dot_general(
            columns, omega, (((0,), (0,)), ((), ())), preferred_element_type=jnp.float32
        ),
        "space",
        scatter_dimension=0,
        tiled=True,
    )
    local_gram = jnp.dot(own_rows.T, own_rows, precision=lax.Precision.HIGHEST)
    gram = lax.psum(local_gram, ("space", "tm"))
    lower = jnp.linalg.cholesky(gram)
    scale = math.sqrt(all_hours)
    solved = jax.scipy.linalg.solve_triangular(lower, own_rows.T, lower=True)
    return (solved.T * scale, lower.T / scale)


def solution(mesh):
    placed = (P("space", None, "tm"), P("space", None, None))
    return jax.shard_map(
        body, mesh=mesh, in_specs=placed, out_specs=(P(("tm", "space"), None), P()), check_vma=False
    )
```

profile of v0, /device:TPU:1, one launch (start us, length us, event | category | flops | bytes accessed | tf_op | source)
XLA Modules:
  0.0 612.2 jit_solution(4493810724609084221)
XLA Ops:
  7.2 3.1 fusion.118
  10.3 4.5 collective-permute-start
  14.9 1.6 collective-permute-start.1
  16.4 45.0 %collective-permute-done = bf16[6,1440,120]{2,1,0:T(8,128)(2,1)S(1)} collective-permute-done((bf16[6,1440,120]{2,1,0:T(8,128)(2,1)S(1)}, bf16[6,1440,120]{2,1,0:T(8,128)(2,1)S(1)}, u32[]{:S(2)}, u32[]{:S(2)}) %collective-permute-start) | collective-permute-done | bytes 2073632 | tf_op jit(solution)/shard_map/ppermute | solution.py:23
  61.4 4.3 collective-permute-done.1
  65.8 7.0 %pad_maximum_fusion.1 = bf16[6,1440,496]{2,1,0:T(8,128)(2,1)S(1)} fusion(bf16[6,1440,120]{2,1,0:T(8,128)(2,1)S(1)} %collective-permute-done.1, bf16[6,1440,256]{2,1,0:T(8,128)(2,1)} %param.3, bf16[6,1440,120]{2,1,0:T(8,128)(2,1)S(1)} %collective-permute-done), kind=kLoop, calls=%fused_computation.16 | loop fusion | flops 25712640 | bytes 17141760 | tf_op jit(solution)/shard_map/concatenate | solution.py:25
  73.2 4.8 collective-permute-start.2
  78.0 2.5 collective-permute-start.3
  80.5 29.6 %collective-permute-done.2 = bf16[2,1440,496]{2,1,0:T(8,128)(2,1)S(1)} collective-permute-done((bf16[2,1440,496]{2,1,0:T(8,128)(2,1)S(1)}, bf16[2,1440,496]{2,1,0:T(8,128)(2,1)S(1)}, u32[]{:S(2)}, u32[]{:S(2)}) %collective-permute-start.2) | collective-permute-done | bytes 2856992 | tf_op jit(solution)/shard_map/ppermute | solution.py:23
  110.1 4.7 collective-permute-done.3
  114.8 13.6 %maximum_maximum_fusion = (bf16[8,1440,496]{2,1,0:T(8,128)(2,1)}, bf16[8,1440,496]{2,1,0:T(8,128)(2,1)}) fusion(bf16[6,1440,120]{2,1,0:T(8,128)(2,1)S(1)} %collective-permute-done.1, bf16[6,1440,256]{2,1,0:T(8,128)(2,1)S(1)} %bitcast.60, bf16[6,1440,120]{2,1,0:T(8,128)(2,1)S(1)} %collective-permute-done, ...), kind=kLoop, calls=%fused_computation.12 | loop fusion | flops 91422720 | bytes 37140480 | tf_op jit(solution)/shard_map/concatenate | solution.py:25
  128.4 16.6 %multiply_add_fusion = f32[6,1440,496]{2,1,0:T(8,128)S(1)} fusion(bf16[8,1440,496]{2,1,0:T(8,128)(2,1)} %get-tuple-element.32, bf16[8,1440,496]{2,1,0:T(8,128)(2,1)} %get-tuple-element.31, bf16[6,1440,120]{2,1,0:T(8,128)(2,1)} %copy-done.1, bf16[6,1440,256]{2,1,0:T(8,128)(2,1)S(1)} %bitcast.62, bf16[6,1440,120]{2,1,0:T(8,128)(2,1)S(1)} %collective-permute-done), kind=kLoop, calls=%fused_computation.11 | loop fusion | flops 81423360 | bytes 59996160 | tf_op jit(solution)/shard_map/add | solution.py:45
  145.0 12.7 %fusion.113 = (f32[6,1438,496]{2,1,0:T(8,128)}, f32[6,1438,496]{2,1,0:T(8,128)}) fusion(f32[6,1440,496]{2,1,0:T(8,128)S(1)} %multiply_add_fusion), kind=kLoop, calls=%fused_computation.198 | loop fusion | bytes 68471808 | tf_op jit(solution)/shard_map/jit(_roll_static)/slice | solution.py:48
  157.8 14.7 %fusion.115 = (f32[6,1439,496]{2,1,0:T(8,128)}, f32[6,1439,496]{2,1,0:T(8,128)}) fusion(f32[6,1440,496]{2,1,0:T(8,128)S(1)} %multiply_add_fusion), kind=kLoop, calls=%fused_computation.200 | loop fusion | bytes 68519424 | tf_op jit(solution)/shard_map/jit(_roll_static)/slice | solution.py:48
  172.5 32.4 %fusion.4 = bf16[6,1440,496]{2,1,0:T(8,128)(2,1)S(1)} fusion(f32[6,1438,496]{2,1,0:T(8,128)} %get-tuple-element.24, f32[6,2,496]{2,1,0:T(2,128)S(1)} %get-tuple-element.26, f32[6,1439,496]{2,1,0:T(8,128)} %get-tuple-element.28, f32[6,1,496]{2,1,0:T(1,128)S(1)} %get-tuple-element.30, f32[6,1,496]{2,1,0:T(1,128)S(1)} %get-tuple-element.29, ...), kind=kLoop, calls=%fused_computation.7 | loop fusion | flops 59996160 | bytes 94279680 | tf_op jit(solution)/shard_map/convert_element_type | solution.py:49
  204.9 7.8 %multiply_reduce_fusion = (f32[8640]{0:T(1024)S(1)}, f32[8640,256]{1,0:T(8,128)}) fusion(bf16[8640,496]{1,0:T(8,128)(2,1)S(1)} %bitcast.64), kind=kOutput, calls=%fused_computation.18 | convolution fusion | flops 2217205248 | bytes 17452800 | tf_op jit(solution)/shard_map/dot_general | solution.py:59
  212.6 12.5 %psum.14 = f32[8640]{0:T(1024)S(1)} all-reduce(f32[8640]{0:T(1024)S(1)} %get-tuple-element.49), channel_id=1, replica_groups=mesh['space'=32,'tm'=4] {'tm'}, use_global_device_ids=true, to_apply=%region_1.3 | all-reduce | flops 8640 | bytes 69120 | tf_op jit(solution)/shard_map/psum | solution.py:61
  225.2 11.7 %fusion.6 = f32[256,512]{1,0:T(8,128)} fusion(bf16[8640,512]{1,0:T(8,128)(2,1)} %bitcast.63, f32[8640,256]{1,0:T(8,128)} %get-tuple-element.50, f32[8640]{0:T(1024)S(1)} %add_rsqrt_fusion), kind=kOutput, calls=%fused_computation.19 | convolution fusion | flops 2269347840 | bytes 18253568 | tf_op jit(solution)/shard_map/dot_general | solution.py:70
  237.2 76.7 %reduce-scatter.2.cloned.1.call-done = f32[8,512]{1,0:T(8,128)} async-done(((f32[256,512]{1,0:T(8,128)}), f32[8,512]{1,0:T(8,128)}) %reduce-scatter.2.cloned.1.call-update) | async-done | bytes 16400 | tf_op jit(solution)/shard_map/reduce_scatter | solution.py:69
  313.9 2.8 fusion.119
  316.8 150.9 %all-reduce.3.cloned.1.call-done = f32[512,512]{0,1:T(8,128)} async-done(((f32[512,512]{0,1:T(8,128)}), f32[512,512]{0,1:T(8,128)}) %all-reduce.3.cloned.1.call-update) | async-done | bytes 1048592 | tf_op jit(solution)/shard_map/psum | solution.py:78
  467.6 1.6 copy.5
  469.2 1.4 fusion.8
  470.7 11.7 %cholesky.104 = f32[128,128]{1,0:T(8,128)S(1)} custom-call(f32[128,128]{1,0:T(8,128)S(1)} %cholesky.266), custom_call_target="Cholesky" | custom-call | tf_op jit(solution)/shard_map/jit(cholesky)/cholesky | solution.py:79
  482.5 9.8 %custom-call.31 = f32[1,128,128]{1,2,0:T(8,128)S(1)} custom-call(f32[1,128,128]{2,1,0:T(8,128)S(1)} %get-tuple-element.48), custom_call_target="InvertDiagBlocksLowerTriangular" | custom-call | tf_op jit(solution)/shard_map/jit(cholesky)/cholesky | solution.py:79
  493.0 11.7 %cholesky.217 = f32[128,128]{1,0:T(8,128)S(1)} custom-call(f32[128,128]{1,0:T(8,128)S(1)} %cholesky.270), custom_call_target="Cholesky" | custom-call | tf_op jit(solution)/shard_map/jit(cholesky)/cholesky | solution.py:79
  504.8 10.0 %custom-call.32 = f32[1,128,128]{1,2,0:T(8,128)S(1)} custom-call(f32[1,128,128]{2,1,0:T(8,128)S(1)} %get-tuple-element.45), custom_call_target="InvertDiagBlocksLowerTriangular" | custom-call | tf_op jit(solution)/shard_map/jit(cholesky)/cholesky | solution.py:79
  515.4 11.7 %cholesky.238 = f32[128,128]{1,0:T(8,128)S(1)} custom-call(f32[128,128]{1,0:T(8,128)S(1)} %cholesky.275), custom_call_target="Cholesky" | custom-call | tf_op jit(solution)/shard_map/jit(cholesky)/cholesky | solution.py:79
  527.9 9.8 %custom-call.33 = f32[1,128,128]{1,2,0:T(8,128)S(1)} custom-call(f32[1,128,128]{2,1,0:T(8,128)S(1)} %get-tuple-element.42), custom_call_target="InvertDiagBlocksLowerTriangular" | custom-call | tf_op jit(solution)/shard_map/jit(cholesky)/cholesky | solution.py:79
  538.3 11.9 %cholesky.255 = f32[128,128]{1,0:T(8,128)S(1)} custom-call(f32[128,128]{1,0:T(8,128)S(1)} %convolution_subtract_fusion.2), custom_call_target="Cholesky" | custom-call | tf_op jit(solution)/shard_map/jit(cholesky)/cholesky | solution.py:79
  555.7 8.0 %while.1 = (s32[]{:T(128)}, f32[512,512]{1,0:T(8,128)S(1)}, s32[4,2]{0,1:T(2,128)S(1)}, f32[4,128,128]{2,1,0:T(8,128)S(1)}, s32[]{:T(128)}) while((s32[]{:T(128)}, f32[512,512]{1,0:T(8,128)S(1)}, s32[4,2]{0,1:T(2,128)S(1)}, f32[4,128,128]{2,1,0:T(8,128)S(1)}, s32[]{:T(128)}) %tuple.42), condition=%wide.while_cond, body=%wide.while_body.sunk | while | flops 2 | bytes 131181 | solution.py:81
  563.7 39.3 %custom-call.34 = f32[4,128,128]{1,2,0:T(8,128)S(1)} custom-call(f32[4,128,128]{2,1,0:T(8,128)S(1)} %get-tuple-element.10), custom_call_target="InvertDiagBlocksLowerTriangular" | custom-call | tf_op jit(solution)/shard_map/jit(_solve_triangular)/triangular_solve | solution.py:81
  (66 shorter events, 16.6 us)
Async XLA Ops:
  7.2 107.6 %slice-start = ((s8[4423680]{0:T(1024)(128)(4,1)}), s8[229376]{0:T(1024)(128)(4,1)S(1)}, s32[]{:S(2)}) async-start(s8[4423680]{0:T(1024)(128)(4,1)} %bitcast.59), calls=%async_computation.3 | async-start | bytes 458752
  7.2 306.7 %reduce-scatter.2.cloned.1.call-start = ((), (), s32[]{:S(2)}) async-start(), calls=%async_computation.1 | async-start | bytes 540672 | tf_op jit(solution)/shard_map/reduce_scatter | solution.py:69
  10.3 51.1 %collective-permute-start = (bf16[6,1440,120]{2,1,0:T(8,128)(2,1)S(1)}, bf16[6,1440,120]{2,1,0:T(8,128)(2,1)S(1)}, u32[]{:S(2)}, u32[]{:S(2)}) collective-permute-start(bf16[6,1440,120]{2,1,0:T(8,128)(2,1)S(1)} %get-tuple-element.35), channel_id=1, source_target_pairs={{0,1},{1,2},{2,3},{4,5},{5,6},{6,7},{8,9},{9,10},{10,11},{12,13},{... | collective-permute-start | bytes 6220808 | tf_op jit(solution)/shard_map/ppermute | solution.py:23
  14.8 99.9 %slice-start.1 = ((s8[4423680]{0:T(1024)(128)(4,1)}), s8[4194304]{0:T(1024)(128)(4,1)S(1)}, s32[]{:S(2)}) async-start(s8[4423680]{0:T(1024)(128)(4,1)} %bitcast.59), calls=%async_computation.4 | async-start | bytes 8388608
  14.9 50.9 %collective-permute-start.1 = (bf16[6,1440,120]{2,1,0:T(8,128)(2,1)S(1)}, bf16[6,1440,120]{2,1,0:T(8,128)(2,1)S(1)}, u32[]{:S(2)}, u32[]{:S(2)}) collective-permute-start(bf16[6,1440,120]{2,1,0:T(8,128)(2,1)S(1)} %get-tuple-element.36), channel_id=1, source_target_pairs={{1,0},{2,1},{3,2},{5,4},{6,5},{7,6},{9,8},{10,9},{11,10},{13,12},{... | collective-permute-start | bytes 6220808 | tf_op jit(solution)/shard_map/ppermute | solution.py:24
  65.8 62.7 %copy-start.1 = (bf16[6,1440,120]{2,1,0:T(8,128)(2,1)}, bf16[6,1440,120]{2,1,0:T(8,128)(2,1)S(1)}, u32[]{:S(2)}) copy-start(bf16[6,1440,120]{2,1,0:T(8,128)(2,1)S(1)} %collective-permute-done.1) | copy-start | bytes 6220804
  73.2 36.9 %collective-permute-start.2 = (bf16[2,1440,496]{2,1,0:T(8,128)(2,1)S(1)}, bf16[2,1440,496]{2,1,0:T(8,128)(2,1)S(1)}, u32[]{:S(2)}, u32[]{:S(2)}) collective-permute-start(bf16[2,1440,496]{2,1,0:T(8,128)(2,1)S(1)} %get-tuple-element.33), channel_id=1, source_target_pairs={{0,4},{4,8},{8,12},{12,16},{16,20},{20,24},{24,28},{28,32},{32,36}... | collective-permute-start | bytes 8570888 | tf_op jit(solution)/shard_map/ppermute | solution.py:23
  78.0 50.4 %slice-start.2 = ((s8[4423680]{0:T(1024)(128)(4,1)}), s8[4194304]{0:T(1024)(128)(4,1)S(1)}, s32[]{:S(2)}) async-start(s8[4423680]{0:T(1024)(128)(4,1)} %bitcast.61), calls=%async_computation.5 | async-start | bytes 8388608
  78.0 50.4 %slice-start.3 = ((s8[4423680]{0:T(1024)(128)(4,1)}), s8[229376]{0:T(1024)(128)(4,1)S(1)}, s32[]{:S(2)}) async-start(s8[4423680]{0:T(1024)(128)(4,1)} %bitcast.61), calls=%async_computation.6 | async-start | bytes 458752
  78.0 36.7 %collective-permute-start.3 = (bf16[2,1440,496]{2,1,0:T(8,128)(2,1)S(1)}, bf16[2,1440,496]{2,1,0:T(8,128)(2,1)S(1)}, u32[]{:S(2)}, u32[]{:S(2)}) collective-permute-start(bf16[2,1440,496]{2,1,0:T(8,128)(2,1)S(1)} %get-tuple-element.34), channel_id=1, source_target_pairs={{4,0},{8,4},{12,8},{16,12},{20,16},{24,20},{28,24},{32,28},{36,32}... | collective-permute-start | bytes 8570888 | tf_op jit(solution)/shard_map/ppermute | solution.py:24
  145.0 27.5 %copy-start = (f32[6,1440,496]{2,1,0:T(8,128)}, f32[6,1440,496]{2,1,0:T(8,128)S(1)}, u32[]{:S(2)}) copy-start(f32[6,1440,496]{2,1,0:T(8,128)S(1)} %multiply_add_fusion) | copy-start | bytes 51425284
  236.9 230.7 %all-reduce.3.cloned.1.call-start = ((), (), s32[]{:S(2)}) async-start(), calls=%async_computation.2 | async-start | bytes 2097152 | tf_op jit(solution)/shard_map/psum | solution.py:78
  313.9 289.1 %copy-start.2 = (f32[8,512]{1,0:T(8,128)S(1)}, f32[8,512]{1,0:T(8,128)}, u32[]{:S(2)}) copy-start(f32[8,512]{1,0:T(8,128)} %reduce-scatter.2.cloned.1.call-done) | copy-start | bytes 49156
Sparse Core Ops, SparseCore 0:
  237.1 76.7 reduce-scatter.1
  319.3 148.3 all-reduce.2
where the time goes:
time: 616 us; the launch traced here: 612 us
  waiting for transfers between devices  311 us (50%)
  other arithmetic  190 us (31%)
  local copies, waits for them, and re-layouts  42 us (7%)
  matrix products  25.6 us (4%)
  between operations  17.1 us (3%)
  starting transfers between devices  13.6 us (2%)
  blocking collectives  12.5 us (2%)
    psum x1, waiting for transfers between devices, body(): gram = lax.psum(local_gram, ('space', 'tm'))  151 us
    another operation x14, other arithmetic, body(): lower = jnp.linalg.cholesky(gram)  78.8 us
    reduce_scatter x1, waiting for transfers between devices, body(): lax.psum_scatter(lax.dot_general(columns, omega, (((0,), (0,)), ((), ()))...  76.7 us
    ppermute x2, waiting for transfers between devices, padded_2(): before = lax.ppermute(last, axis, up)  74.6 us
    another operation x2, other arithmetic, body(): solved = jax.scipy.linalg.solve_triangular(lower, own_rows.T, lower=True)  39.3 us
    convert_element_type x1, other arithmetic, smooth_rows(): return total.astype(jnp.bfloat16)  32.4 us
    slice x4, local copies, waits for them, and re-layouts, smooth_rows(): total = total + smooth_taps[shift] * jnp.roll(across, 2 - shift, axis=1)  27.5 us
    concatenate x2, other arithmetic, padded_2(): x = jnp.concatenate([before, x, after], axis=dim)  20.7 us
  transfers between devices with their start and end apart: 6, of which 6 were waited for; matrix products, arithmetic and copies ran while one was open for 0% of the time, Pallas kernels for 0%

commit v1 on v0

--- a/solution.py
+++ b/solution.py
@@ -1,11 +1,17 @@
+import functools
 import math
 
 import jax
 import jax.numpy as jnp
 from jax import lax
+from jax.experimental import pallas as pl
+from jax.experimental.pallas import tpu as pltpu
 from jax.sharding import PartitionSpec as P
 
 HALO = 120
+F32 = jnp.float32
+HI = lax.Precision.HIGHEST
+MESH = pl.DeviceIdType.MESH
 
 
 low_cutoff = 1.0 / 240.0
@@ -47,6 +53,178 @@
     for shift in (0, 1, 3, 4):
         total = total + smooth_taps[shift] * jnp.roll(across, 2 - shift, axis=1)
     return total.astype(jnp.bfloat16)
+
+
+def gather_kernel(part_ref, all_ref, own_ref, arrived, send_sem, recv_sem, out_sem, in_sem, pair_sem):
+    spaces, blocks = lax.axis_size("space"), lax.axis_size("tm")
+    chips = spaces // 2
+    flat = chips * blocks
+    s, t = lax.axis_index("space"), lax.axis_index("tm")
+    core, chip = lax.rem(s, 2), s // 2
+    sibling = 2 * chip + 1 - core
+    mine = chip * blocks + t
+    rows = own_ref.shape[0]
+
+    def across(q):
+        return lax.rem(s + q, spaces), t
+
+    def around(e):
+        to = lax.rem(mine + e, flat)
+        return 2 * (to // blocks) + core, lax.rem(to, blocks)
+
+    barrier = pltpu.get_barrier_semaphore()
+
+    @pl.loop(1, spaces)
+    def _(q):
+        pl.semaphore_signal(barrier, inc=1, device_id=across(q), device_id_type=MESH)
+
+    @pl.loop(1, flat)
+    def _(e):
+        pl.semaphore_signal(barrier, inc=1, device_id=around(e), device_id_type=MESH)
+
+    pl.semaphore_wait(barrier, spaces + flat - 2)
+
+    @pl.loop(1, spaces)
+    def _(q):
+        to, _ = across(q)
+        pltpu.make_async_remote_copy(
+            src_ref=part_ref.at[pl.ds(pl.multiple_of(to * rows, rows), rows)],
+            dst_ref=arrived.at[q - 1],
+            send_sem=send_sem,
+            recv_sem=recv_sem,
+            device_id=across(q),
+            device_id_type=MESH,
+        ).start()
+
+    landed = pltpu.make_async_copy(arrived, arrived, recv_sem)
+    landed.wait()
+    total = part_ref[pl.ds(pl.multiple_of(s * rows, rows), rows), :]
+    for q in range(spaces - 1):
+        total = total + arrived[q]
+    own_ref[...] = total
+    all_ref[core, mine] = total
+
+    @pl.loop(1, flat)
+    def _(e):
+        pltpu.make_async_remote_copy(
+            src_ref=own_ref,
+            dst_ref=all_ref.at[core, mine],
+            send_sem=out_sem,
+            recv_sem=in_sem,
+            device_id=around(e),
+            device_id_type=MESH,
+        ).start()
+
+    others = all_ref.at[core, pl.ds(0, flat - 1)]
+    pltpu.make_async_copy(others, others, in_sem).wait()
+    pair = pltpu.make_async_remote_copy(
+        src_ref=all_ref.at[core],
+        dst_ref=all_ref.at[core],
+        send_sem=pair_sem.at[0],
+        recv_sem=pair_sem.at[1],
+        device_id=(sibling, t),
+        device_id_type=MESH,
+    )
+    pair.start()
+    pltpu.make_async_copy(arrived, arrived, send_sem).wait()
+    pltpu.make_async_copy(others, others, out_sem).wait()
+    pair.wait()
+
+
+def gather(part, spaces, blocks):
+    hours, n = part.shape
+    rows = hours // spaces
+    flat = spaces // 2 * blocks
+    vmem = pl.BlockSpec(memory_space=pltpu.VMEM)
+    return pl.pallas_call(
+        gather_kernel,
+        out_shape=(
+            jax.ShapeDtypeStruct((2, flat, rows, n), F32),
+            jax.ShapeDtypeStruct((rows, n), F32),
+        ),
+        in_specs=[vmem],
+        out_specs=(vmem, vmem),
+        scratch_shapes=[
+            pltpu.VMEM((spaces - 1, rows, n), F32),
+            pltpu.SemaphoreType.DMA,
+            pltpu.SemaphoreType.DMA,
+            pltpu.SemaphoreType.DMA,
+            pltpu.SemaphoreType.DMA,
+            pltpu.SemaphoreType.DMA((2,)),
+        ],
+        compiler_params=pltpu.CompilerParams(
+            collective_id=0, has_side_effects=True, vmem_limit_bytes=32 * 2**20
+        ),
+        name="gather",
+    )(part)
+
+
+def factor_block(m_ref):
+    lane8 = lax.broadcasted_iota(jnp.int32, (8, 1), 0)
+    for q in range(16):
+        top = 8 * q
+        p = m_ref[top:top + 8, :]
+        cols = [jnp.broadcast_to(m_ref[top:128, top + k:top + k + 1], (128 - top, 128)) for k in range(8)]
+        scaled = []
+        for k in range(8):
+            c = cols[k]
+            d = c[k:k + 1, :]
+            r = 1.0 / d
+            for m in range(k + 1, 8):
+                cols[m] = cols[m] - c * (cols[m][k:k + 1, :] * r)
+            row = p[k:k + 1, :]
+            t = row * jnp.concatenate([r, r], axis=1)
+            below = jnp.where(lane8 > k, c[0:8, :], 0.0)
+            p = p - jnp.concatenate([below, below], axis=1) * t
+            scaled.append(t)
+            s = lax.rsqrt(d)
+            m_ref[top + k:top + k + 1, :] = row * jnp.concatenate([s, s], axis=1)
+        if q < 15:
+            left = m_ref[top + 8:128, 0:128]
+            right = m_ref[top + 8:128, 128:256]
+            for k in range(8):
+                c = cols[k][8:, :]
+                left = left - c * scaled[k][:, 0:128]
+                right = right - c * scaled[k][:, 128:256]
+            m_ref[top + 8:128, 0:128] = left
+            m_ref[top + 8:128, 128:256] = right
+
+def factor_kernel(root, y_ref, own_ref, basis_ref, r_ref, a_ref, m_ref, rest_ref):
+    n = y_ref.shape[1]
+    blocks = n // 128
+    a_ref[...] = lax.dot_general(y_ref[...], y_ref[...], (((0,), (0,)), ((), ())), precision=HI, preferred_element_type=F32)
+    rest_ref[...] = own_ref[...]
+    row = lax.broadcasted_iota(jnp.int32, (128, 128), 0)
+    col = lax.broadcasted_iota(jnp.int32, (128, 128), 1)
+
+    @pl.loop(0, blocks)
+    def _(b):
+        here = pl.ds(pl.multiple_of(b * 128, 128), 128)
+        m_ref[:, 0:128] = a_ref[here, here]
+        m_ref[:, 128:256] = (row == col).astype(F32)
+        factor_block(m_ref)
+        inv = m_ref[:, 128:256]
+        x = lax.dot_general(rest_ref[:, here], inv, (((1,), (1,)), ((), ())), precision=HI, preferred_element_type=F32)
+        basis_ref[:, here] = x * root
+        panel = jnp.dot(inv, a_ref[here, :], precision=HI, preferred_element_type=F32)
+        wide = lax.broadcasted_iota(jnp.int32, (128, n), 1) >= (b + 1) * 128
+        panel = jnp.where(wide, panel, 0.0)
+        r_ref[here, :] = panel * (1.0 / root)
+        r_ref[here, here] = jnp.where(row <= col, m_ref[:, 0:128], 0.0) * (1.0 / root)
+        rest_ref[...] -= jnp.dot(x, panel, precision=HI, preferred_element_type=F32)
+        a_ref[...] -= lax.dot_general(panel, panel, (((0,), (0,)), ((), ())), precision=HI, preferred_element_type=F32)
+
+def factor(y, own, hours):
+    n = y.shape[1]
+    return pl.pallas_call(
+        functools.partial(factor_kernel, math.sqrt(hours)),
+        out_shape=(jax.ShapeDtypeStruct((own.shape[0], n), F32), jax.ShapeDtypeStruct((n, n), F32)),
+        in_specs=[pl.BlockSpec(memory_space=pltpu.VMEM)] * 2,
+        out_specs=(pl.BlockSpec(memory_space=pltpu.VMEM), pl.BlockSpec(memory_space=pltpu.VMEM)),
+        scratch_shapes=[pltpu.VMEM((n, n), F32), pltpu.VMEM((128, 256), F32), pltpu.VMEM((own.shape[0], n), F32)],
+        compiler_params=pltpu.CompilerParams(vmem_limit_bytes=32 * 2**20),
+        name="factor",
+    )(y, own)
 
 
 def body(field, sketch):
@@ -66,20 +244,9 @@
     columns = lax.slice_in_dim(
         standard, 0, lax.axis_size("space") * (block_hours // lax.axis_size("space")), axis=1
     )
-    own_rows = lax.psum_scatter(
-        lax.dot_general(
-            columns, omega, (((0,), (0,)), ((), ())), preferred_element_type=jnp.float32
-        ),
-        "space",
-        scatter_dimension=0,
-        tiled=True,
-    )
-    local_gram = jnp.dot(own_rows.T, own_rows, precision=lax.Precision.HIGHEST)
-    gram = lax.psum(local_gram, ("space", "tm"))
-    lower = jnp.linalg.cholesky(gram)
-    scale = math.sqrt(all_hours)
-    solved = jax.scipy.linalg.solve_triangular(lower, own_rows.T, lower=True)
-    return (solved.T * scale, lower.T / scale)
+    part = lax.dot_general(columns, omega, (((0,), (0,)), ((), ())), preferred_element_type=jnp.float32)
+    everyone, own = gather(part, lax.axis_size("space"), lax.axis_size("tm"))
+    return factor(everyone.reshape(all_hours, -1), own, all_hours)
 
 
 def solution(mesh):

time: 616 us -> 294 us (0.48)
  waiting for transfers between devices: 311 us -> 83.7 us
  other arithmetic: 190 us -> 69.3 us
  Pallas kernels: 0 us -> 60.8 us
  between operations: 17.1 us -> 0.94 us
  local copies, waits for them, and re-layouts: 42 us -> 34.4 us
  matrix products: 25.6 us -> 18.7 us
    psum x1 -> x0, waiting for transfers between devices: 151 us -> none  [body(): gram = lax.psum(local_gram, ('space', 'tm'))]
    another operation x16 -> x0, other arithmetic: 118 us -> none  [the longest x14 78.8 us: body(): lower = jnp.linalg.cholesky(gram)]
    reduce_scatter x1 -> x0, waiting for transfers between devices: 76.7 us -> none  [body(): lax.psum_scatter(lax.dot_general(columns, omega, (((0,), (0,)), ((), ()))...]
    pallas_call x0 -> x2, Pallas kernels: none -> 60.8 us  [the longest x1 37.7 us: gather(): pl.pallas_call(gather_kernel, out_shape=(jax.ShapeDtypeStruct((2, flat, r...]
    another operation x17 -> x0, local copies, waits for them, and re-layouts: 8.1 us -> none
  transfers between devices with their start and end apart: 6 -> 4, of which waited for: 6 -> 4; matrix products, arithmetic and copies ran while one was open for 0% -> 0% of each run, Pallas kernels for 0% -> 0%
where the time goes in v1:
time: 294 us; the launch traced here: 293 us
  waiting for transfers between devices  83.7 us (28%)
  other arithmetic  69.3 us (24%)
  Pallas kernels  60.8 us (21%)
  local copies, waits for them, and re-layouts  34.4 us (12%)
  matrix products  18.7 us (6%)
  starting transfers between devices  12.8 us (4%)
  blocking collectives  12.5 us (4%)
    ppermute x2, waiting for transfers between devices, padded_2(): before = lax.ppermute(last, axis, up)  75.4 us
    pallas_call x1, Pallas kernels, gather(): pl.pallas_call(gather_kernel, out_shape=(jax.ShapeDtypeStruct((2, flat, r...  37.7 us
    convert_element_type x1, other arithmetic, smooth_rows(): return total.astype(jnp.bfloat16)  32.2 us
    slice x4, local copies, waits for them, and re-layouts, smooth_rows(): total = total + smooth_taps[shift] * jnp.roll(across, 2 - shift, axis=1)  25.4 us
    pallas_call x1, Pallas kernels, factor(): pl.pallas_call(functools.partial(factor_kernel, math.sqrt(hours)), out_sh...  23.1 us
    concatenate x2, other arithmetic, padded_2(): x = jnp.concatenate([before, x, after], axis=dim)  20.6 us
    add x1, other arithmetic, smooth_rows(): across + smooth_taps[shift] * padded[shift:shift + count].astype(jnp.floa...  16.5 us
    psum x1, blocking collectives, body(): energy = lax.psum(jnp.sum(wide * wide, axis=1), 'tm')  12.5 us
  transfers between devices with their start and end apart: 4, of which 4 were waited for; matrix products, arithmetic and copies ran while one was open for 0% of the time, Pallas kernels for 0%

profile of v1, /device:TPU:1, one launch (start us, length us, event | category | flops | bytes accessed | tf_op | source)
XLA Modules:
  0.0 293.3 jit_solution(12925546333558507983)
XLA Ops:
  0.6 0.0 slice-start
  0.6 3.2 %fusion.85 = (bf16[6,1440,120]{2,1,0:T(8,128)(2,1)S(1)}, bf16[6,1440,120]{2,1,0:T(8,128)(2,1)S(1)}) fusion(bf16[6,1440,256]{2,1,0:T(8,128)(2,1)} %param.3), kind=kLoop, calls=%fused_computation.133 | loop fusion | bytes 8294400 | tf_op jit(solution)/shard_map/slice | solution.py:27
  3.8 4.5 %collective-permute-start = (bf16[6,1440,120]{2,1,0:T(8,128)(2,1)S(1)}, bf16[6,1440,120]{2,1,0:T(8,128)(2,1)S(1)}, u32[]{:S(2)}, u32[]{:S(2)}) collective-permute-start(bf16[6,1440,120]{2,1,0:T(8,128)(2,1)S(1)} %get-tuple-element.19), channel_id=1, source_target_pairs={{0,1},{1,2},{2,3},{4,5},{5,6},{6,7},{8,9},{9,10},{10,11},{12,13},{... | collective-permute-start | bytes 6220808 | tf_op jit(solution)/shard_map/ppermute | solution.py:29
  8.4 0.0 slice-start.1
  8.4 1.4 collective-permute-start.1
  9.8 45.2 %collective-permute-done = bf16[6,1440,120]{2,1,0:T(8,128)(2,1)S(1)} collective-permute-done((bf16[6,1440,120]{2,1,0:T(8,128)(2,1)S(1)}, bf16[6,1440,120]{2,1,0:T(8,128)(2,1)S(1)}, u32[]{:S(2)}, u32[]{:S(2)}) %collective-permute-start) | collective-permute-done | bytes 2073632 | tf_op jit(solution)/shard_map/ppermute | solution.py:29
  55.0 4.2 %collective-permute-done.1 = bf16[6,1440,120]{2,1,0:T(8,128)(2,1)S(1)} collective-permute-done((bf16[6,1440,120]{2,1,0:T(8,128)(2,1)S(1)}, bf16[6,1440,120]{2,1,0:T(8,128)(2,1)S(1)}, u32[]{:S(2)}, u32[]{:S(2)}) %collective-permute-start.1) | collective-permute-done | bytes 2073632 | tf_op jit(solution)/shard_map/ppermute | solution.py:30
  59.1 0.0 copy-start.1
  59.1 7.0 %pad_maximum_fusion.1 = bf16[6,1440,496]{2,1,0:T(8,128)(2,1)S(1)} fusion(bf16[6,1440,120]{2,1,0:T(8,128)(2,1)S(1)} %collective-permute-done.1, bf16[6,1440,256]{2,1,0:T(8,128)(2,1)} %param.3, bf16[6,1440,120]{2,1,0:T(8,128)(2,1)S(1)} %collective-permute-done), kind=kLoop, calls=%fused_computation.14 | loop fusion | flops 25712640 | bytes 17141760 | tf_op jit(solution)/shard_map/concatenate | solution.py:31
  66.2 2.2 fusion.84
  68.3 4.8 %collective-permute-start.2 = (bf16[2,1440,496]{2,1,0:T(8,128)(2,1)}, bf16[2,1440,496]{2,1,0:T(8,128)(2,1)S(1)}, u32[]{:S(2)}, u32[]{:S(2)}) collective-permute-start(bf16[2,1440,496]{2,1,0:T(8,128)(2,1)} %get-tuple-element.17), channel_id=1, source_target_pairs={{0,4},{4,8},{8,12},{12,16},{16,20},{20,24},{24,28},{28,32},{32,36}... | collective-permute-start | bytes 8570888 | tf_op jit(solution)/shard_map/ppermute | solution.py:29
  73.2 2.1 collective-permute-start.3
  75.3 30.3 %collective-permute-done.2 = bf16[2,1440,496]{2,1,0:T(8,128)(2,1)S(1)} collective-permute-done((bf16[2,1440,496]{2,1,0:T(8,128)(2,1)}, bf16[2,1440,496]{2,1,0:T(8,128)(2,1)S(1)}, u32[]{:S(2)}, u32[]{:S(2)}) %collective-permute-start.2) | collective-permute-done | bytes 2856992 | tf_op jit(solution)/shard_map/ppermute | solution.py:29
  105.6 4.1 %collective-permute-done.3 = bf16[2,1440,496]{2,1,0:T(8,128)(2,1)S(1)} collective-permute-done((bf16[2,1440,496]{2,1,0:T(8,128)(2,1)S(1)}, bf16[2,1440,496]{2,1,0:T(8,128)(2,1)S(1)}, u32[]{:S(2)}, u32[]{:S(2)}) %collective-permute-start.3) | collective-permute-done | bytes 2856992 | tf_op jit(solution)/shard_map/ppermute | solution.py:30
  109.6 0.0 slice-done
  109.6 0.0 slice-done.1
  109.6 13.6 %maximum_maximum_fusion = (bf16[8,1440,496]{2,1,0:T(8,128)(2,1)}, bf16[8,1440,496]{2,1,0:T(8,128)(2,1)}) fusion(bf16[6,1440,120]{2,1,0:T(8,128)(2,1)S(1)} %collective-permute-done.1, bf16[6,1440,256]{2,1,0:T(8,128)(2,1)S(1)} %bitcast.7, bf16[6,1440,120]{2,1,0:T(8,128)(2,1)S(1)} %collective-permute-done, bf16[2,1440,496]{2,1,0:T(8,128)(2,1)S(1)} %collective-permute-done.2, ...), kind=kLoop, calls=%fused_computation.10 | loop fusion | flops 91422720 | bytes 37140480 | tf_op jit(solution)/shard_map/concatenate | solution.py:31
  123.2 0.0 copy-done.1
  123.2 16.5 %multiply_add_fusion = f32[6,1440,496]{2,1,0:T(8,128)S(1)} fusion(bf16[8,1440,496]{2,1,0:T(8,128)(2,1)} %get-tuple-element.16, bf16[8,1440,496]{2,1,0:T(8,128)(2,1)} %get-tuple-element.15, bf16[6,1440,120]{2,1,0:T(8,128)(2,1)} %copy-done.1, bf16[6,1440,256]{2,1,0:T(8,128)(2,1)S(1)} %bitcast.7, bf16[6,1440,120]{2,1,0:T(8,128)(2,1)S(1)} %collective-permute-done), kind=kLoop, calls=%fused_computation.9 | loop fusion | flops 81423360 | bytes 59996160 | tf_op jit(solution)/shard_map/add | solution.py:51
  139.8 0.0 copy-start
  139.9 12.9 %fusion.80 = (f32[6,1438,496]{2,1,0:T(8,128)}, f32[6,1438,496]{2,1,0:T(8,128)}) fusion(f32[6,1440,496]{2,1,0:T(8,128)S(1)} %multiply_add_fusion), kind=kLoop, calls=%fused_computation.128 | loop fusion | bytes 68471808 | tf_op jit(solution)/shard_map/jit(_roll_static)/slice | solution.py:54
  152.8 3.6 %copy-done = f32[6,1440,496]{2,1,0:T(8,128)} copy-done((f32[6,1440,496]{2,1,0:T(8,128)}, f32[6,1440,496]{2,1,0:T(8,128)S(1)}, u32[]{:S(2)}) %copy-start) | copy-done | bytes 17141784
  156.4 12.4 %fusion.82 = (f32[6,1439,496]{2,1,0:T(8,128)}, f32[6,1439,496]{2,1,0:T(8,128)}) fusion(f32[6,1440,496]{2,1,0:T(8,128)S(1)} %multiply_add_fusion), kind=kLoop, calls=%fused_computation.130 | loop fusion | bytes 68519424 | tf_op jit(solution)/shard_map/jit(_roll_static)/slice | solution.py:54
  168.8 32.2 %fusion.4 = bf16[6,1440,496]{2,1,0:T(8,128)(2,1)S(1)} fusion(f32[6,1438,496]{2,1,0:T(8,128)} %get-tuple-element.8, f32[6,2,496]{2,1,0:T(2,128)S(1)} %get-tuple-element.10, f32[6,1439,496]{2,1,0:T(8,128)} %get-tuple-element.12, f32[6,1,496]{2,1,0:T(1,128)S(1)} %get-tuple-element.14, f32[6,1,496]{2,1,0:T(1,128)S(1)} %get-tuple-element.13, ...), kind=kLoop, calls=%fused_computation.5 | loop fusion | flops 59996160 | bytes 94279680 | tf_op jit(solution)/shard_map/convert_element_type | solution.py:55
  201.0 7.8 %multiply_reduce_fusion = (f32[8640]{0:T(1024)S(1)}, f32[8640,256]{1,0:T(8,128)}) fusion(bf16[8640,496]{1,0:T(8,128)(2,1)S(1)} %bitcast.9), kind=kOutput, calls=%fused_computation.16 | convolution fusion | flops 2217205248 | bytes 17452800 | tf_op jit(solution)/shard_map/dot_general | solution.py:237
  208.8 12.5 %psum.7 = f32[8640]{0:T(1024)S(1)} all-reduce(f32[8640]{0:T(1024)S(1)} %get-tuple-element.21), channel_id=1, replica_groups=mesh['space'=32,'tm'=4] {'tm'}, use_global_device_ids=true, to_apply=%region_1.3 | all-reduce | flops 8640 | bytes 69120 | tf_op jit(solution)/shard_map/psum | solution.py:239
  221.4 10.9 %fusion.6.part_ref = f32[256,512]{1,0:T(8,128)S(1)} fusion(bf16[8640,512]{1,0:T(8,128)(2,1)} %bitcast.8, f32[8640,256]{1,0:T(8,128)} %get-tuple-element.22, f32[8640]{0:T(1024)S(1)} %add_rsqrt_fusion), kind=kOutput, calls=%fused_computation.17 | convolution fusion | flops 2269347840 | bytes 18253568 | tf_op jit(solution)/shard_map/dot_general | solution.py:247
  232.3 37.7 %gather.1 = (f32[2,64,8,512]{3,2,1,0:T(8,128)S(1)}, f32[8,512]{1,0:T(8,128)S(1)}) custom-call(f32[256,512]{1,0:T(8,128)S(1)} %fusion.6.part_ref), custom_call_target="tpu_custom_call" | custom-call | tf_op jit(solution)/shard_map/gather/pallas_call | solution.py:139
  270.0 23.1 %factor.1 = (f32[8,512]{1,0:T(8,128)}, f32[512,512]{1,0:T(8,128)}) custom-call(f32[1024,512]{1,0:T(8,128)S(1)} %bitcast.5, f32[8,512]{1,0:T(8,128)S(1)} %get-tuple-element.6.own_ref), custom_call_target="tpu_custom_call" | custom-call | tf_op jit(solution)/shard_map/factor/pallas_call | solution.py:219
  (4 shorter events, 0.1 us)
Async XLA Ops:
  0.6 109.0 %slice-start = ((s8[4423680]{0:T(1024)(128)(4,1)}), s8[4194304]{0:T(1024)(128)(4,1)S(1)}, s32[]{:S(2)}) async-start(s8[4423680]{0:T(1024)(128)(4,1)} %bitcast.6), calls=%async_computation | async-start | bytes 8388608
  3.8 51.1 %collective-permute-start = (bf16[6,1440,120]{2,1,0:T(8,128)(2,1)S(1)}, bf16[6,1440,120]{2,1,0:T(8,128)(2,1)S(1)}, u32[]{:S(2)}, u32[]{:S(2)}) collective-permute-start(bf16[6,1440,120]{2,1,0:T(8,128)(2,1)S(1)} %get-tuple-element.19), channel_id=1, source_target_pairs={{0,1},{1,2},{2,3},{4,5},{5,6},{6,7},{8,9},{9,10},{10,11},{12,13},{... | collective-permute-start | bytes 6220808 | tf_op jit(solution)/shard_map/ppermute | solution.py:29
  8.4 101.3 %slice-start.1 = ((s8[4423680]{0:T(1024)(128)(4,1)}), s8[229376]{0:T(1024)(128)(4,1)S(1)}, s32[]{:S(2)}) async-start(s8[4423680]{0:T(1024)(128)(4,1)} %bitcast.6), calls=%async_computation.1 | async-start | bytes 458752
  8.4 50.8 %collective-permute-start.1 = (bf16[6,1440,120]{2,1,0:T(8,128)(2,1)S(1)}, bf16[6,1440,120]{2,1,0:T(8,128)(2,1)S(1)}, u32[]{:S(2)}, u32[]{:S(2)}) collective-permute-start(bf16[6,1440,120]{2,1,0:T(8,128)(2,1)S(1)} %get-tuple-element.20), channel_id=1, source_target_pairs={{1,0},{2,1},{3,2},{5,4},{6,5},{7,6},{9,8},{10,9},{11,10},{13,12},{... | collective-permute-start | bytes 6220808 | tf_op jit(solution)/shard_map/ppermute | solution.py:30
  59.1 64.1 %copy-start.1 = (bf16[6,1440,120]{2,1,0:T(8,128)(2,1)}, bf16[6,1440,120]{2,1,0:T(8,128)(2,1)S(1)}, u32[]{:S(2)}) copy-start(bf16[6,1440,120]{2,1,0:T(8,128)(2,1)S(1)} %collective-permute-done.1) | copy-start | bytes 6220804
  68.3 37.2 %collective-permute-start.2 = (bf16[2,1440,496]{2,1,0:T(8,128)(2,1)}, bf16[2,1440,496]{2,1,0:T(8,128)(2,1)S(1)}, u32[]{:S(2)}, u32[]{:S(2)}) collective-permute-start(bf16[2,1440,496]{2,1,0:T(8,128)(2,1)} %get-tuple-element.17), channel_id=1, source_target_pairs={{0,4},{4,8},{8,12},{12,16},{16,20},{20,24},{24,28},{28,32},{32,36}... | collective-permute-start | bytes 8570888 | tf_op jit(solution)/shard_map/ppermute | solution.py:29
  73.2 36.5 %collective-permute-start.3 = (bf16[2,1440,496]{2,1,0:T(8,128)(2,1)S(1)}, bf16[2,1440,496]{2,1,0:T(8,128)(2,1)S(1)}, u32[]{:S(2)}, u32[]{:S(2)}) collective-permute-start(bf16[2,1440,496]{2,1,0:T(8,128)(2,1)S(1)} %get-tuple-element.18), channel_id=1, source_target_pairs={{4,0},{8,4},{12,8},{16,12},{20,16},{24,20},{28,24},{32,28},{36,32}... | collective-permute-start | bytes 8570888 | tf_op jit(solution)/shard_map/ppermute | solution.py:30
  139.8 16.6 %copy-start = (f32[6,1440,496]{2,1,0:T(8,128)}, f32[6,1440,496]{2,1,0:T(8,128)S(1)}, u32[]{:S(2)}) copy-start(f32[6,1440,496]{2,1,0:T(8,128)S(1)} %multiply_add_fusion) | copy-start | bytes 51425284

commit v2 on v1

--- a/solution.py
+++ b/solution.py
@@ -3,6 +3,7 @@
 
 import jax
 import jax.numpy as jnp
+import numpy as np
 from jax import lax
 from jax.experimental import pallas as pl
 from jax.experimental.pallas import tpu as pltpu
@@ -19,40 +20,284 @@
 smooth_taps = (1.0 / 16.0, 4.0 / 16.0, 6.0 / 16.0, 4.0 / 16.0, 1.0 / 16.0)
 
 
-def padded_2(x, sides, width):
-    for axis, dim in sides:
-        devices, length = (lax.axis_size(axis), x.shape[dim])
-        up = [(i, (i + 1) % devices) for i in range(devices - 1)]
-        down = [(j, i) for i, j in up]
-        last = lax.slice_in_dim(x, length - width, length, axis=dim)
-        leading = lax.slice_in_dim(x, 0, width, axis=dim)
-        before = lax.ppermute(last, axis, up)
-        after = lax.ppermute(leading, axis, down)
-        x = jnp.concatenate([before, x, after], axis=dim)
-    return x
-
-
-def band_matrix(span):
-    rows_idx = jnp.arange(span + 2 * HALO, dtype=jnp.float32)
-    cols_idx = jnp.arange(span, dtype=jnp.float32)
-    offset = rows_idx[:, None] - cols_idx[None, :] - HALO
-    value = 2.0 * high_cutoff * jnp.sinc(2.0 * high_cutoff * offset) - 2.0 * low_cutoff * jnp.sinc(
-        2.0 * low_cutoff * offset
+def band_weights(span):
+    m = np.arange(span + 256, dtype=np.float64)[None, :] - 128.0 - np.arange(span, dtype=np.float64)[:, None]
+    value = 2.0 * high_cutoff * np.sinc(2.0 * high_cutoff * m) - 2.0 * low_cutoff * np.sinc(2.0 * low_cutoff * m)
+    value = value * np.sinc(m / (HALO + 1.0))
+    return np.where(np.abs(m) <= HALO, value, 0.0).astype(np.float32).astype(jnp.bfloat16)
+
+
+def ring_weights(piece):
+    offset = np.arange(piece + 32)[None, :] - 16 - np.arange(piece)[:, None]
+    value = np.zeros(offset.shape, np.float32)
+    for shift in range(-2, 3):
+        value = np.where(offset == shift, smooth_taps[shift + 2], value)
+    return value.astype(jnp.bfloat16)
+
+
+def front_kernel(
+    hours,
+    field_ref,
+    sketch_ref,
+    band_ref,
+    ring_ref,
+    part_ref,
+    x,
+    series,
+    omega,
+    filtered,
+    energy,
+    heard,
+    load_sem,
+    omega_sem,
+    row_sem,
+    rim_sem,
+    energy_out,
+    energy_in,
+):
+    spaces, blocks = lax.axis_size("space"), lax.axis_size("tm")
+    s, t = lax.axis_index("space"), lax.axis_index("tm")
+    rows, lon, span = field_ref.shape
+    piece = ring_ref.shape[0]
+    last = rows + 2
+
+    own = pltpu.make_async_copy(field_ref, x.at[2:last, 16 : lon + 16], load_sem.at[0])
+    left = pltpu.make_async_copy(field_ref.at[:, lon - 16 : lon], x.at[2:last, 0:16], load_sem.at[1])
+    right = pltpu.make_async_copy(field_ref.at[:, 0:16], x.at[2:last, lon + 16 : lon + 32], load_sem.at[2])
+    own.start()
+    left.start()
+    right.start()
+    load_omega = pltpu.make_async_copy(sketch_ref, omega, omega_sem)
+
+    barrier = pltpu.get_barrier_semaphore()
+    for q in range(1, blocks):
+        pl.semaphore_signal(barrier, inc=1, device_id=(s, lax.rem(t + q, blocks)), device_id_type=MESH)
+
+    @pl.when(s > 0)
+    def _():
+        pl.semaphore_signal(barrier, inc=1, device_id=(s - 1, t), device_id_type=MESH)
+
+    @pl.when(s < spaces - 1)
+    def _():
+        pl.semaphore_signal(barrier, inc=1, device_id=(s + 1, t), device_id_type=MESH)
+
+    pl.semaphore_wait(barrier, blocks - 1 + jnp.where(s > 0, 1, 0) + jnp.where(s < spaces - 1, 1, 0))
+
+    up = pltpu.make_async_remote_copy(
+        src_ref=field_ref.at[rows - 2 : rows],
+        dst_ref=x.at[0:2, 16 : lon + 16],
+        send_sem=row_sem.at[0],
+        recv_sem=row_sem.at[1],
+        device_id=(s + 1, t),
+        device_id_type=MESH,
     )
-    value = value * jnp.sinc(offset / (HALO + 1.0))
-    inside = jnp.abs(offset) <= HALO
-    return jnp.where(inside, value, jnp.zeros_like(value)).astype(jnp.bfloat16)
-
-
-def smooth_rows(padded):
-    count = padded.shape[0] - 4
-    across = smooth_taps[0] * padded[0:count].astype(jnp.float32)
-    for shift in range(1, 5):
-        across = across + smooth_taps[shift] * padded[shift : shift + count].astype(jnp.float32)
-    total = smooth_taps[2] * across
-    for shift in (0, 1, 3, 4):
-        total = total + smooth_taps[shift] * jnp.roll(across, 2 - shift, axis=1)
-    return total.astype(jnp.bfloat16)
+    down = pltpu.make_async_remote_copy(
+        src_ref=field_ref.at[0:2],
+        dst_ref=x.at[last : last + 2, 16 : lon + 16],
+        send_sem=row_sem.at[2],
+        recv_sem=row_sem.at[3],
+        device_id=(s - 1, t),
+        device_id_type=MESH,
+    )
+
+    @pl.when(s < spaces - 1)
+    def _():
+        up.start()
+
+    @pl.when(s > 0)
+    def _():
+        down.start()
+
+    own.wait()
+    left.wait()
+    right.wait()
+    load_omega.start()
+
+    def smooth(first):
+        @pl.loop(0, lon // piece)
+        def _(c):
+            at = pl.multiple_of(c * piece, 16)
+            across = [
+                jnp.dot(ring_ref[...], x[first + r, pl.ds(at, piece + 32), :], preferred_element_type=F32)
+                for r in range(6)
+            ]
+            for r in range(2):
+                total = smooth_taps[2] * across[r + 2] + smooth_taps[1] * (across[r + 1] + across[r + 3])
+                total = total + smooth_taps[0] * (across[r] + across[r + 4])
+                series[first + r, pl.ds(at, piece), 128 : 128 + span] = total.astype(jnp.bfloat16)
+
+    def rims(i):
+        before = pltpu.make_async_remote_copy(
+            src_ref=series.at[i, :, span : span + 128],
+            dst_ref=series.at[i, :, 0:128],
+            send_sem=rim_sem.at[0, i],
+            recv_sem=rim_sem.at[1, i],
+            device_id=(s, t + 1),
+            device_id_type=MESH,
+        )
+        after = pltpu.make_async_remote_copy(
+            src_ref=series.at[i, :, 128:256],
+            dst_ref=series.at[i, :, span + 128 : span + 256],
+            send_sem=rim_sem.at[2, i],
+            recv_sem=rim_sem.at[3, i],
+            device_id=(s, t - 1),
+            device_id_type=MESH,
+        )
+        return before, after
+
+    def send_rims(first):
+        for r in range(2):
+            before, after = rims(first + r)
+
+            @pl.when(t < blocks - 1)
+            def _():
+                before.start()
+
+            @pl.when(t > 0)
+            def _():
+                after.start()
+
+    smooth(2)
+    send_rims(2)
+
+    @pl.when(t == 0)
+    def _():
+        series[:, :, 0:128] = jnp.zeros((rows, lon, 128), jnp.bfloat16)
+
+    @pl.when(t == blocks - 1)
+    def _():
+        series[:, :, span + 128 : span + 256] = jnp.zeros((rows, lon, 128), jnp.bfloat16)
+
+    @pl.when(s < spaces - 1)
+    def _():
+        down.wait_recv()
+
+    @pl.when(s == spaces - 1)
+    def _():
+        x[last : last + 2, 16 : lon + 16] = jnp.zeros((2, lon, span), jnp.bfloat16)
+
+    x[last : last + 2, 0:16] = x[last : last + 2, lon : lon + 16]
+    x[last : last + 2, lon + 16 : lon + 32] = x[last : last + 2, 16:32]
+    smooth(4)
+    send_rims(4)
+
+    @pl.when(s > 0)
+    def _():
+        up.wait_recv()
+
+    @pl.when(s == 0)
+    def _():
+        x[0:2, 16 : lon + 16] = jnp.zeros((2, lon, span), jnp.bfloat16)
+
+    x[0:2, 0:16] = x[0:2, lon : lon + 16]
+    x[0:2, lon + 16 : lon + 32] = x[0:2, 16:32]
+    smooth(0)
+    send_rims(0)
+
+    def energy_copy(i, q):
+        return pltpu.make_async_remote_copy(
+            src_ref=energy.at[i],
+            dst_ref=heard.at[i, q - 1],
+            send_sem=energy_out.at[i],
+            recv_sem=energy_in.at[i],
+            device_id=(s, lax.rem(t + q, blocks)),
+            device_id_type=MESH,
+        )
+
+    def filter_row(i):
+        before, after = rims(i)
+
+        @pl.when(t > 0)
+        def _():
+            before.wait_recv()
+
+        @pl.when(t < blocks - 1)
+        def _():
+            after.wait_recv()
+
+        value = lax.dot_general(
+            band_ref[...], series[i], (((1,), (1,)), ((), ())), preferred_element_type=F32
+        ).astype(jnp.bfloat16)
+        filtered[i] = value
+        wide = value.astype(F32)
+        energy[i] = jnp.sum(wide * wide, axis=0, keepdims=True)
+        for q in range(1, blocks):
+            energy_copy(i, q).start()
+
+    def sketch_row(i):
+        pltpu.make_async_copy(heard.at[i], heard.at[i], energy_in.at[i]).wait()
+        total = energy[i]
+        for q in range(blocks - 1):
+            total = total + heard[i, q]
+        inverse = lax.rsqrt(total / hours + 1e-06)
+        standard = (filtered[i].astype(F32) * inverse).astype(jnp.bfloat16)
+        part_ref[...] += jnp.dot(standard, omega[i], preferred_element_type=F32)
+
+    part_ref[...] = jnp.zeros(part_ref.shape, F32)
+    load_omega.wait()
+
+    @pl.loop(0, rows + 1)
+    def _(n):
+        @pl.when(n < rows)
+        def _():
+            filter_row(lax.rem(n + 2, rows))
+
+        @pl.when(n > 0)
+        def _():
+            sketch_row(lax.rem(n + 1, rows))
+
+    @pl.when(s < spaces - 1)
+    def _():
+        up.wait_send()
+
+    @pl.when(s > 0)
+    def _():
+        down.wait_send()
+
+    for i in range(rows):
+        before, after = rims(i)
+
+        @pl.when(t < blocks - 1)
+        def _():
+            before.wait_send()
+
+        @pl.when(t > 0)
+        def _():
+            after.wait_send()
+
+        pltpu.make_async_copy(heard.at[i], heard.at[i], energy_out.at[i]).wait()
+
+
+def front(field, sketch, spaces, blocks):
+    rows, lon, span = field.shape
+    n = sketch.shape[2]
+    piece = 144
+    vmem = pl.BlockSpec(memory_space=pltpu.VMEM)
+    hbm = pl.BlockSpec(memory_space=pl.ANY)
+    return pl.pallas_call(
+        functools.partial(front_kernel, span * blocks),
+        out_shape=jax.ShapeDtypeStruct((span, n), F32),
+        in_specs=[hbm, hbm, vmem, vmem],
+        out_specs=vmem,
+        scratch_shapes=[
+            pltpu.VMEM((rows + 4, lon + 32, span), jnp.bfloat16),
+            pltpu.VMEM((rows, lon, span + 256), jnp.bfloat16),
+            pltpu.VMEM((rows, lon, n), jnp.bfloat16),
+            pltpu.VMEM((rows, span, lon), jnp.bfloat16),
+            pltpu.VMEM((rows, 1, lon), F32),
+            pltpu.VMEM((rows, blocks - 1, 1, lon), F32),
+            pltpu.SemaphoreType.DMA((3,)),
+            pltpu.SemaphoreType.DMA,
+            pltpu.SemaphoreType.DMA((4,)),
+            pltpu.SemaphoreType.DMA((4, rows)),
+            pltpu.SemaphoreType.DMA((rows,)),
+            pltpu.SemaphoreType.DMA((rows,)),
+        ],
+        compiler_params=pltpu.CompilerParams(
+            collective_id=1, has_side_effects=True, vmem_limit_bytes=56 * 2**20
+        ),
+        name="front",
+    )(field, sketch, jnp.asarray(band_weights(span)), jnp.asarray(ring_weights(piece)))
 
 
 def gather_kernel(part_ref, all_ref, own_ref, arrived, send_sem, recv_sem, out_sem, in_sem, pair_sem):
@@ -228,24 +473,10 @@
 
 
 def body(field, sketch):
-    block_hours = field.shape[2]
-    widened = padded_2(field, (("tm", 2),), HALO)
-    taller = padded_2(widened, (("space", 0),), 2)
-    smooth = smooth_rows(taller)
-    flat = smooth.reshape(-1, block_hours + 2 * HALO)
-    band = band_matrix(block_hours)
-    filtered = jnp.dot(flat, band, preferred_element_type=jnp.float32).astype(jnp.bfloat16)
-    wide = filtered.astype(jnp.float32)
-    energy = lax.psum(jnp.sum(wide * wide, axis=1), "tm")
-    all_hours = block_hours * lax.axis_size("tm")
-    inverse = lax.rsqrt(energy / all_hours + 1e-06)
-    standard = (wide * inverse[:, None]).astype(jnp.bfloat16)
-    omega = sketch.reshape(-1, sketch.shape[2])
-    columns = lax.slice_in_dim(
-        standard, 0, lax.axis_size("space") * (block_hours // lax.axis_size("space")), axis=1
-    )
-    part = lax.dot_general(columns, omega, (((0,), (0,)), ((), ())), preferred_element_type=jnp.float32)
-    everyone, own = gather(part, lax.axis_size("space"), lax.axis_size("tm"))
+    spaces, blocks = lax.axis_size("space"), lax.axis_size("tm")
+    all_hours = field.shape[2] * blocks
+    part = front(field, sketch, spaces, blocks)
+    everyone, own = gather(part, spaces, blocks)
     return factor(everyone.reshape(all_hours, -1), own, all_hours)
 
 

time: 294 us -> 131 us (0.45)
  waiting for transfers between devices: 83.7 us -> 0 us
  other arithmetic: 69.3 us -> 0 us
  Pallas kernels: 60.8 us -> 129 us
  local copies, waits for them, and re-layouts: 34.4 us -> 1.03 us
  matrix products: 18.7 us -> 0 us
  starting transfers between devices: 12.8 us -> 0 us
  blocking collectives: 12.5 us -> 0 us
    ppermute x4 -> x0, waiting for transfers between devices: 83.7 us -> none  [the longest x2 75.4 us: padded_2(): before = lax.ppermute(last, axis, up)]
    pallas_call x0 -> x1, Pallas kernels: none -> 70.1 us  [front(): pl.pallas_call(functools.partial(front_kernel, span * blocks), out_shape=...]
    convert_element_type x1 -> x0, other arithmetic: 32.2 us -> none  [smooth_rows(): return total.astype(jnp.bfloat16)]
    slice x6 -> x0, local copies, waits for them, and re-layouts: 30.8 us -> none  [the longest x4 25.4 us: smooth_rows(): total = total + smooth_taps[shift] * jnp.roll(across, 2 - shift, axis=1)]
    concatenate x2 -> x0, other arithmetic: 20.6 us -> none  [padded_2(): x = jnp.concatenate([before, x, after], axis=dim)]
    dot_general x2 -> x0, matrix products: 18.7 us -> none  [the longest x1 10.9 us: body(): lax.dot_general(columns, omega, (((0,), (0,)), ((), ())), preferred_eleme...]
    add x1 -> x0, other arithmetic: 16.5 us -> none  [smooth_rows(): across + smooth_taps[shift] * padded[shift:shift + count].astype(jnp.floa...]
    ppermute x4 -> x0, starting transfers between devices: 12.8 us -> none  [the longest x2 9.32 us: padded_2(): before = lax.ppermute(last, axis, up)]
  transfers between devices with their start and end apart: 4 -> 0, of which waited for: 4 -> 0; matrix products, arithmetic and copies ran while one was open for 0% -> 0% of each run, Pallas kernels for 0% -> 0%
where the time goes in v2:
time: 131 us; the launch traced here: 130 us
  Pallas kernels  129 us (98%)
    pallas_call x1, Pallas kernels, front(): pl.pallas_call(functools.partial(front_kernel, span * blocks), out_shape=...  70.1 us
    pallas_call x1, Pallas kernels, gather(): pl.pallas_call(gather_kernel, out_shape=(jax.ShapeDtypeStruct((2, flat, r...  35.5 us
    pallas_call x1, Pallas kernels, factor(): pl.pallas_call(functools.partial(factor_kernel, math.sqrt(hours)), out_sh...  23.1 us

profile of v2, /device:TPU:1, one launch (start us, length us, event | category | flops | bytes accessed | tf_op | source)
XLA Modules:
  0.0 130.4 jit_solution(7590950062608806354)
XLA Ops:
  0.6 70.1 %front.1.part_ref = f32[256,512]{1,0:T(8,128)} custom-call(bf16[6,1440,256]{2,1,0:T(8,128)(2,1)} %field_ref.1, bf16[6,1440,512]{2,1,0:T(8,128)(2,1)} %sketch_ref.1, bf16[256,512]{1,0:T(8,128)(2,1)} %constant.4.clone.band_ref, bf16[144,176]{1,0:T(8,128)(2,1)} %constant.5.clone.ring_ref), custom_call_target="tpu_custom_call" | custom-call | tf_op jit(solution)/shard_map/front/pallas_call | solution.py:277
  70.7 0.0 copy-start
  70.7 1.0 copy-done
  71.8 35.5 %gather.1 = (f32[2,64,8,512]{3,2,1,0:T(8,128)S(1)}, f32[8,512]{1,0:T(8,128)S(1)}) custom-call(f32[256,512]{1,0:T(8,128)S(1)} %copy-done), custom_call_target="tpu_custom_call" | custom-call | tf_op jit(solution)/shard_map/gather/pallas_call | solution.py:384
  107.3 23.1 %factor.1 = (f32[8,512]{1,0:T(8,128)}, f32[512,512]{1,0:T(8,128)}) custom-call(f32[1024,512]{1,0:T(8,128)S(1)} %bitcast.1, f32[8,512]{1,0:T(8,128)S(1)} %get-tuple-element.5.own_ref), custom_call_target="tpu_custom_call" | custom-call | tf_op jit(solution)/shard_map/factor/pallas_call | solution.py:464
Async XLA Ops:
  70.7 1.0 copy-start

commit v3 on v2

--- a/solution.py
+++ b/solution.py
@@ -41,7 +41,8 @@
     sketch_ref,
     band_ref,
     ring_ref,
-    part_ref,
+    all_ref,
+    own_ref,
     x,
     series,
     omega,
@@ -54,12 +55,29 @@
     rim_sem,
     energy_out,
     energy_in,
+    part,
+    offered,
+    arrived,
+    mine_ref,
+    sum_sem,
+    gather_sem,
+    pair_sem,
 ):
     spaces, blocks = lax.axis_size("space"), lax.axis_size("tm")
     s, t = lax.axis_index("space"), lax.axis_index("tm")
     rows, lon, span = field_ref.shape
     piece = ring_ref.shape[0]
     last = rows + 2
+    core, chip = lax.rem(s, 2), s // 2
+    flat = spaces // 2 * blocks
+    mine = chip * blocks + t
+
+    def across(q):
+        return lax.rem(s + q, spaces), t
+
+    def around(e):
+        to = lax.rem(mine + e, flat)
+        return 2 * (to // blocks) + core, lax.rem(to, blocks)
 
     own = pltpu.make_async_copy(field_ref, x.at[2:last, 16 : lon + 16], load_sem.at[0])
     left = pltpu.make_async_copy(field_ref.at[:, lon - 16 : lon], x.at[2:last, 0:16], load_sem.at[1])
@@ -70,18 +88,16 @@
     load_omega = pltpu.make_async_copy(sketch_ref, omega, omega_sem)
 
     barrier = pltpu.get_barrier_semaphore()
-    for q in range(1, blocks):
-        pl.semaphore_signal(barrier, inc=1, device_id=(s, lax.rem(t + q, blocks)), device_id_type=MESH)
-
-    @pl.when(s > 0)
-    def _():
-        pl.semaphore_signal(barrier, inc=1, device_id=(s - 1, t), device_id_type=MESH)
-
-    @pl.when(s < spaces - 1)
-    def _():
-        pl.semaphore_signal(barrier, inc=1, device_id=(s + 1, t), device_id_type=MESH)
-
-    pl.semaphore_wait(barrier, blocks - 1 + jnp.where(s > 0, 1, 0) + jnp.where(s < spaces - 1, 1, 0))
+
+    @pl.loop(1, spaces)
+    def _(q):
+        pl.semaphore_signal(barrier, inc=1, device_id=across(q), device_id_type=MESH)
+
+    @pl.loop(1, flat)
+    def _(e):
+        pl.semaphore_signal(barrier, inc=1, device_id=around(e), device_id_type=MESH)
+
+    pl.semaphore_wait(barrier, spaces + flat - 2)
 
     up = pltpu.make_async_remote_copy(
         src_ref=field_ref.at[rows - 2 : rows],
@@ -231,9 +247,9 @@
             total = total + heard[i, q]
         inverse = lax.rsqrt(total / hours + 1e-06)
         standard = (filtered[i].astype(F32) * inverse).astype(jnp.bfloat16)
-        part_ref[...] += jnp.dot(standard, omega[i], preferred_element_type=F32)
-
-    part_ref[...] = jnp.zeros(part_ref.shape, F32)
+        part[...] += jnp.dot(standard, omega[i], preferred_element_type=F32)
+
+    part[...] = jnp.zeros(part.shape, F32)
     load_omega.wait()
 
     @pl.loop(0, rows + 1)
@@ -246,6 +262,57 @@
         def _():
             sketch_row(lax.rem(n + 1, rows))
 
+    half = part.shape[1] // 2
+    split = part[...].reshape(spaces, span // spaces, 2 * half)
+    offered[...] = jnp.concatenate([split[:, :, :half], split[:, :, half:]], axis=1).astype(jnp.bfloat16)
+
+    @pl.loop(1, spaces)
+    def _(q):
+        to, _ = across(q)
+        pltpu.make_async_remote_copy(
+            src_ref=offered.at[to],
+            dst_ref=arrived.at[q - 1],
+            send_sem=sum_sem.at[0],
+            recv_sem=sum_sem.at[1],
+            device_id=across(q),
+            device_id_type=MESH,
+        ).start()
+
+    near = part[pl.ds(pl.multiple_of(s * 8, 8), 8), :]
+    pltpu.make_async_copy(arrived, arrived, sum_sem.at[1]).wait()
+    total = jnp.concatenate([near[:, :half], near[:, half:]], axis=0)
+    for q in range(spaces - 1):
+        total = total + arrived[q].astype(F32)
+    own_ref[:, :half] = total[:8]
+    own_ref[:, half:] = total[8:]
+    mine_ref[...] = total.astype(jnp.bfloat16)
+    all_ref[core, mine] = total.astype(jnp.bfloat16)
+
+    @pl.loop(1, flat)
+    def _(e):
+        pltpu.make_async_remote_copy(
+            src_ref=mine_ref,
+            dst_ref=all_ref.at[core, mine],
+            send_sem=gather_sem.at[0],
+            recv_sem=gather_sem.at[1],
+            device_id=around(e),
+            device_id_type=MESH,
+        ).start()
+
+    others = all_ref.at[core, pl.ds(0, flat - 1)]
+    pltpu.make_async_copy(others, others, gather_sem.at[1]).wait()
+    pair = pltpu.make_async_remote_copy(
+        src_ref=all_ref.at[core],
+        dst_ref=all_ref.at[core],
+        send_sem=pair_sem.at[0],
+        recv_sem=pair_sem.at[1],
+        device_id=(2 * chip + 1 - core, t),
+        device_id_type=MESH,
+    )
+    pair.start()
+    pltpu.make_async_copy(arrived, arrived, sum_sem.at[0]).wait()
+    pltpu.make_async_copy(others, others, gather_sem.at[0]).wait()
+
     @pl.when(s < spaces - 1)
     def _():
         up.wait_send()
@@ -266,6 +333,8 @@
             after.wait_send()
 
         pltpu.make_async_copy(heard.at[i], heard.at[i], energy_out.at[i]).wait()
+
+    pair.wait()
 
 
 def front(field, sketch, spaces, blocks):
@@ -276,9 +345,12 @@
     hbm = pl.BlockSpec(memory_space=pl.ANY)
     return pl.pallas_call(
         functools.partial(front_kernel, span * blocks),
-        out_shape=jax.ShapeDtypeStruct((span, n), F32),
+        out_shape=(
+            jax.ShapeDtypeStruct((2, spaces // 2 * blocks, 16, n // 2), jnp.bfloat16),
+            jax.ShapeDtypeStruct((8, n), F32),
+        ),
         in_specs=[hbm, hbm, vmem, vmem],
-        out_specs=vmem,
+        out_specs=(vmem, vmem),
         scratch_shapes=[
             pltpu.VMEM((rows + 4, lon + 32, span), jnp.bfloat16),
             pltpu.VMEM((rows, lon, span + 256), jnp.bfloat16),
@@ -292,116 +364,19 @@
             pltpu.SemaphoreType.DMA((4, rows)),
             pltpu.SemaphoreType.DMA((rows,)),
             pltpu.SemaphoreType.DMA((rows,)),
+            pltpu.VMEM((span, n), F32),
+            pltpu.VMEM((spaces, 16, n // 2), jnp.bfloat16),
+            pltpu.VMEM((spaces - 1, 16, n // 2), jnp.bfloat16),
+            pltpu.VMEM((16, n // 2), jnp.bfloat16),
+            pltpu.SemaphoreType.DMA((2,)),
+            pltpu.SemaphoreType.DMA((2,)),
+            pltpu.SemaphoreType.DMA((2,)),
         ],
         compiler_params=pltpu.CompilerParams(
-            collective_id=1, has_side_effects=True, vmem_limit_bytes=56 * 2**20
+            collective_id=0, has_side_effects=True, vmem_limit_bytes=56 * 2**20
         ),
         name="front",
     )(field, sketch, jnp.asarray(band_weights(span)), jnp.asarray(ring_weights(piece)))
-
-
-def gather_kernel(part_ref, all_ref, own_ref, arrived, send_sem, recv_sem, out_sem, in_sem, pair_sem):
-    spaces, blocks = lax.axis_size("space"), lax.axis_size("tm")
-    chips = spaces // 2
-    flat = chips * blocks
-    s, t = lax.axis_index("space"), lax.axis_index("tm")
-    core, chip = lax.rem(s, 2), s // 2
-    sibling = 2 * chip + 1 - core
-    mine = chip * blocks + t
-    rows = own_ref.shape[0]
-
-    def across(q):
-        return lax.rem(s + q, spaces), t
-
-    def around(e):
-        to = lax.rem(mine + e, flat)
-        return 2 * (to // blocks) + core, lax.rem(to, blocks)
-
-    barrier = pltpu.get_barrier_semaphore()
-
-    @pl.loop(1, spaces)
-    def _(q):
-        pl.semaphore_signal(barrier, inc=1, device_id=across(q), device_id_type=MESH)
-
-    @pl.loop(1, flat)
-    def _(e):
-        pl.semaphore_signal(barrier, inc=1, device_id=around(e), device_id_type=MESH)
-
-    pl.semaphore_wait(barrier, spaces + flat - 2)
-
-    @pl.loop(1, spaces)
-    def _(q):
-        to, _ = across(q)
-        pltpu.make_async_remote_copy(
-            src_ref=part_ref.at[pl.ds(pl.multiple_of(to * rows, rows), rows)],
-            dst_ref=arrived.at[q - 1],
-            send_sem=send_sem,
-            recv_sem=recv_sem,
-            device_id=across(q),
-            device_id_type=MESH,
-        ).start()
-
-    landed = pltpu.make_async_copy(arrived, arrived, recv_sem)
-    landed.wait()
-    total = part_ref[pl.ds(pl.multiple_of(s * rows, rows), rows), :]
-    for q in range(spaces - 1):
-        total = total + arrived[q]
-    own_ref[...] = total
-    all_ref[core, mine] = total
-
-    @pl.loop(1, flat)
-    def _(e):
-        pltpu.make_async_remote_copy(
-            src_ref=own_ref,
-            dst_ref=all_ref.at[core, mine],
-            send_sem=out_sem,
-            recv_sem=in_sem,
-            device_id=around(e),
-            device_id_type=MESH,
-        ).start()
-
-    others = all_ref.at[core, pl.ds(0, flat - 1)]
-    pltpu.make_async_copy(others, others, in_sem).wait()
-    pair = pltpu.make_async_remote_copy(
-        src_ref=all_ref.at[core],
-        dst_ref=all_ref.at[core],
-        send_sem=pair_sem.at[0],
-        recv_sem=pair_sem.at[1],
-        device_id=(sibling, t),
-        device_id_type=MESH,
-    )
-    pair.start()
-    pltpu.make_async_copy(arrived, arrived, send_sem).wait()
-    pltpu.make_async_copy(others, others, out_sem).wait()
-    pair.wait()
-
-
-def gather(part, spaces, blocks):
-    hours, n = part.shape
-    rows = hours // spaces
-    flat = spaces // 2 * blocks
-    vmem = pl.BlockSpec(memory_space=pltpu.VMEM)
-    return pl.pallas_call(
-        gather_kernel,
-        out_shape=(
-            jax.ShapeDtypeStruct((2, flat, rows, n), F32),
-            jax.ShapeDtypeStruct((rows, n), F32),
-        ),
-        in_specs=[vmem],
-        out_specs=(vmem, vmem),
-        scratch_shapes=[
-            pltpu.VMEM((spaces - 1, rows, n), F32),
-            pltpu.SemaphoreType.DMA,
-            pltpu.SemaphoreType.DMA,
-            pltpu.SemaphoreType.DMA,
-            pltpu.SemaphoreType.DMA,
-            pltpu.SemaphoreType.DMA((2,)),
-        ],
-        compiler_params=pltpu.CompilerParams(
-            collective_id=0, has_side_effects=True, vmem_limit_bytes=32 * 2**20
-        ),
-        name="gather",
-    )(part)
 
 
 def factor_block(m_ref):
@@ -435,9 +410,11 @@
             m_ref[top + 8:128, 128:256] = right
 
 def factor_kernel(root, y_ref, own_ref, basis_ref, r_ref, a_ref, m_ref, rest_ref):
-    n = y_ref.shape[1]
+    n = own_ref.shape[1]
     blocks = n // 128
-    a_ref[...] = lax.dot_general(y_ref[...], y_ref[...], (((0,), (0,)), ((), ())), precision=HI, preferred_element_type=F32)
+    pairs = y_ref[...].astype(F32)
+    y = jnp.concatenate([pairs[:, :8].reshape(-1, n // 2), pairs[:, 8:].reshape(-1, n // 2)], axis=1).astype(jnp.bfloat16)
+    a_ref[...] = lax.dot_general(y, y, (((0,), (0,)), ((), ())), preferred_element_type=F32)
     rest_ref[...] = own_ref[...]
     row = lax.broadcasted_iota(jnp.int32, (128, 128), 0)
     col = lax.broadcasted_iota(jnp.int32, (128, 128), 1)
@@ -460,7 +437,7 @@
         a_ref[...] -= lax.dot_general(panel, panel, (((0,), (0,)), ((), ())), precision=HI, preferred_element_type=F32)
 
 def factor(y, own, hours):
-    n = y.shape[1]
+    n = own.shape[1]
     return pl.pallas_call(
         functools.partial(factor_kernel, math.sqrt(hours)),
         out_shape=(jax.ShapeDtypeStruct((own.shape[0], n), F32), jax.ShapeDtypeStruct((n, n), F32)),
@@ -475,9 +452,8 @@
 def body(field, sketch):
     spaces, blocks = lax.axis_size("space"), lax.axis_size("tm")
     all_hours = field.shape[2] * blocks
-    part = front(field, sketch, spaces, blocks)
-    everyone, own = gather(part, spaces, blocks)
-    return factor(everyone.reshape(all_hours, -1), own, all_hours)
+    everyone, own = front(field, sketch, spaces, blocks)
+    return factor(everyone.reshape(-1, 16, everyone.shape[3]), own, all_hours)
 
 
 def solution(mesh):

time: 131 us -> 116 us (0.89)
  Pallas kernels: 129 us -> 113 us
    pallas_call x1 -> x0, Pallas kernels: 35.5 us -> none  [gather(): pl.pallas_call(gather_kernel, out_shape=(jax.ShapeDtypeStruct((2, flat, r...]
    pallas_call x1, Pallas kernels: 70.1 us -> 93 us  [front(): pl.pallas_call(functools.partial(front_kernel, span * blocks), out_shape=...]
    pallas_call x1, Pallas kernels: 23.1 us -> 20.3 us  [factor(): pl.pallas_call(functools.partial(factor_kernel, math.sqrt(hours)), out_sh...]
where the time goes in v3:
time: 116 us
  Pallas kernels  113 us (97%)
  local copies, waits for them, and re-layouts  1.93 us (2%)
    pallas_call x1, Pallas kernels, front(): pl.pallas_call(functools.partial(front_kernel, span * blocks), out_shape=...  93 us
    pallas_call x1, Pallas kernels, factor(): pl.pallas_call(functools.partial(factor_kernel, math.sqrt(hours)), out_sh...  20.3 us

profile of v3, /device:TPU:1, one launch (start us, length us, event | category | flops | bytes accessed | tf_op | source)
XLA Modules:
  0.0 115.9 jit_solution(5195151934852807636)
XLA Ops:
  0.6 93.0 %front.1 = (bf16[2,64,16,256]{3,2,1,0:T(8,128)(2,1)}, f32[8,512]{1,0:T(8,128)}) custom-call(bf16[6,1440,256]{2,1,0:T(8,128)(2,1)} %field_ref.1, bf16[6,1440,512]{2,1,0:T(8,128)(2,1)} %sketch_ref.1, bf16[256,512]{1,0:T(8,128)(2,1)} %constant.4.clone.band_ref, bf16[144,176]{1,0:T(8,128)(2,1)} %constant.5.clone.ring_ref), custom_call_target="tpu_custom_call" | custom-call | tf_op jit(solution)/shard_map/front/pallas_call | solution.py:346
  93.6 0.0 copy-start
  93.7 1.2 %copy-done = bf16[2,64,16,256]{3,2,1,0:T(8,128)(2,1)S(1)} copy-done((bf16[2,64,16,256]{3,2,1,0:T(8,128)(2,1)S(1)}, bf16[2,64,16,256]{3,2,1,0:T(8,128)(2,1)}, u32[]{:S(2)}) %copy-start) | copy-done | bytes 1048600
  94.9 0.0 copy-start.1
  94.9 0.7 copy-done.1
  95.6 20.3 %factor.1 = (f32[8,512]{1,0:T(8,128)}, f32[512,512]{1,0:T(8,128)}) custom-call(bf16[128,16,256]{2,1,0:T(8,128)(2,1)S(1)} %bitcast.1, f32[8,512]{1,0:T(8,128)S(1)} %copy-done.1), custom_call_target="tpu_custom_call" | custom-call | tf_op jit(solution)/shard_map/factor/pallas_call | solution.py:441
Async XLA Ops:
  93.6 1.2 %copy-start = (bf16[2,64,16,256]{3,2,1,0:T(8,128)(2,1)S(1)}, bf16[2,64,16,256]{3,2,1,0:T(8,128)(2,1)}, u32[]{:S(2)}) copy-start(bf16[2,64,16,256]{3,2,1,0:T(8,128)(2,1)} %get-tuple-element.4) | copy-start | bytes 3145732
  94.9 0.7 copy-start.1

commit v4 on v3

v4 whole, which is shorter than its diff:
```python
import functools
import math

import jax
import jax.numpy as jnp
import numpy as np
from jax import lax
from jax.experimental import pallas as pl
from jax.experimental.pallas import tpu as pltpu
from jax.sharding import PartitionSpec as P

HALO = 120
F32 = jnp.float32
HI = lax.Precision.HIGHEST
MESH = pl.DeviceIdType.MESH
LAG = 4


low_cutoff = 1.0 / 240.0
high_cutoff = 0.4
smooth_taps = (1.0 / 16.0, 4.0 / 16.0, 6.0 / 16.0, 4.0 / 16.0, 1.0 / 16.0)


def band_weights(span):
    m = np.arange(span + 256, dtype=np.float64)[None, :] - 128.0 - np.arange(span, dtype=np.float64)[:, None]
    value = 2.0 * high_cutoff * np.sinc(2.0 * high_cutoff * m) - 2.0 * low_cutoff * np.sinc(2.0 * low_cutoff * m)
    value = value * np.sinc(m / (HALO + 1.0))
    return np.where(np.abs(m) <= HALO, value, 0.0).astype(np.float32).astype(jnp.bfloat16)


def ring_weights(piece):
    offset = np.arange(piece + 32)[None, :] - 16 - np.arange(piece)[:, None]
    value = np.zeros(offset.shape, np.float32)
    for shift in range(-2, 3):
        value = np.where(offset == shift, smooth_taps[shift + 2], value)
    return value.astype(jnp.bfloat16)


def front_kernel(
    hours,
    field_ref,
    sketch_ref,
    band_ref,
    ring_ref,
    all_ref,
    own_ref,
    x,
    series,
    omega,
    filtered,
    energy,
    heard,
    part,
    offered,
    arrived,
    mine_ref,
    load_sem,
    omega_sem,
    row_sem,
    rim_sem,
    energy_sem,
    sum_sem,
    sent_sem,
    gather_sem,
    pair_sem,
):
    spaces, blocks = lax.axis_size("space"), lax.axis_size("tm")
    s, t = lax.axis_index("space"), lax.axis_index("tm")
    rows, lon, span = field_ref.shape
    piece = ring_ref.shape[0]
    reach = lon // 2
    units = 2 * rows
    last = rows + 2
    chips = spaces // 2
    core, chip = lax.rem(s, 2), s // 2
    flat = chips * blocks
    mine = t * chips + chip

    def across(q):
        return lax.rem(s + q, spaces), t

    def around(e):
        to = lax.rem(mine + e, flat)
        return 2 * lax.rem(to, chips) + core, to // chips

    barrier = pltpu.get_barrier_semaphore()

    own = pltpu.make_async_copy(field_ref, x.at[2:last, 16 : lon + 16], load_sem.at[0])
    left = pltpu.make_async_copy(field_ref.at[:, lon - 16 : lon], x.at[2:last, 0:16], load_sem.at[1])
    right = pltpu.make_async_copy(field_ref.at[:, 0:16], x.at[2:last, lon + 16 : lon + 32], load_sem.at[2])
    own.start()
    left.start()
    right.start()
    load_omega = pltpu.make_async_copy(sketch_ref, omega, omega_sem)

    @pl.loop(1, spaces)
    def _(q):
        pl.semaphore_signal(barrier, inc=1, device_id=across(q), device_id_type=MESH)

    @pl.loop(1, flat)
    def _(e):
        pl.semaphore_signal(barrier, inc=1, device_id=around(e), device_id_type=MESH)

    def halo(part_of, step):
        take = slice(rows - 2, rows) if step > 0 else slice(0, 2)
        give = slice(0, 2) if step > 0 else slice(last, last + 2)
        if part_of == 0:
            wrap, inner = (lon - 16, 0), (0, reach + 16)
        else:
            wrap, inner = (0, lon + 16), (reach + 16, lon)
        sems = 2 * part_of + (0 if step > 0 else 1)
        copies = []
        for low, high, to in (
            (inner[0], inner[1], inner[0] + 16),
            (wrap[0], wrap[0] + 16, wrap[1]),
        ):
            copies.append(
                pltpu.make_async_remote_copy(
                    src_ref=field_ref.at[take, low:high],
                    dst_ref=x.at[give, to : to + high - low],
                    send_sem=row_sem.at[0, sems],
                    recv_sem=row_sem.at[1, sems],
                    device_id=(s + step, t),
                    device_id_type=MESH,
                )
            )
        return copies

    def halo_wait(part_of, step, side):
        give = slice(0, 2) if step > 0 else slice(last, last + 2)
        cut = reach + 32
        whole = x.at[give, 0:cut] if part_of == 0 else x.at[give, cut : lon + 32]
        sems = 2 * part_of + (0 if step > 0 else 1)
        pltpu.make_async_copy(whole, whole, row_sem.at[side, sems]).wait()

    def smooth(first, half):
        @pl.loop(0, reach // piece)
        def _(c):
            at = pl.multiple_of(half * reach + c * piece, 16)
            horizontal = [
                jnp.dot(ring_ref[...], x[first + r, pl.ds(at, piece + 32), :], preferred_element_type=F32)
                for r in range(6)
            ]
            for r in range(2):
                total = smooth_taps[2] * horizontal[r + 2] + smooth_taps[1] * (horizontal[r + 1] + horizontal[r + 3])
                total = total + smooth_taps[0] * (horizontal[r] + horizontal[r + 4])
                series[first + r, pl.ds(at, piece), 128 : 128 + span] = total.astype(jnp.bfloat16)

    def place(u):
        early = u < 4
        half = jnp.where(early, u // 2, (u - 4) // 4)
        row = jnp.where(early, 2 + lax.rem(u, 2), lax.rem(u, 4) + 4 - 6 * (lax.rem(u, 4) // 2))
        return row, pl.ds(pl.multiple_of(half * reach, 16), reach)

    def rims(u):
        row, where = place(u)
        before = pltpu.make_async_remote_copy(
            src_ref=series.at[row, where, span : span + 128],
            dst_ref=series.at[row, where, 0:128],
            send_sem=rim_sem.at[0, u],
            recv_sem=rim_sem.at[1, u],
            device_id=(s, t + 1),
            device_id_type=MESH,
        )
        after = pltpu.make_async_remote_copy(
            src_ref=series.at[row, where, 128:256],
            dst_ref=series.at[row, where, span + 128 : span + 256],
            send_sem=rim_sem.at[2, u],
            recv_sem=rim_sem.at[3, u],
            device_id=(s, t - 1),
            device_id_type=MESH,
        )
        return before, after

    def send_rims(u):
        before, after = rims(u)

        @pl.when(t < blocks - 1)
        def _():
            before.start()

        @pl.when(t > 0)
        def _():
            after.start()

    def sent_rims(u):
        before, after = rims(u)

        @pl.when(t < blocks - 1)
        def _():
            before.wait_send()

        @pl.when(t > 0)
        def _():
            after.wait_send()

    def filter_unit(u):
        row, where = place(u)
        before, after = rims(u)

        @pl.when(t > 0)
        def _():
            before.wait_recv()

        @pl.when(t < blocks - 1)
        def _():
            after.wait_recv()

        value = lax.dot_general(
            band_ref[...], series[row, where, :], (((1,), (1,)), ((), ())), preferred_element_type=F32
        ).astype(jnp.bfloat16)
        filtered[u] = value
        wide = value.astype(F32)
        energy[u] = jnp.sum(wide * wide, axis=0, keepdims=True)
        for q in range(1, blocks):
            pltpu.make_async_remote_copy(
                src_ref=energy.at[u],
                dst_ref=heard.at[u, q - 1],
                send_sem=energy_sem.at[0, u],
                recv_sem=energy_sem.at[1, u],
                device_id=(s, lax.rem(t + q, blocks)),
                device_id_type=MESH,
            ).start()

    def sketch_unit(u):
        row, where = place(u)
        pltpu.make_async_copy(heard.at[u], heard.at[u], energy_sem.at[1, u]).wait()
        total = energy[u]
        for q in range(blocks - 1):
            total = total + heard[u, q]
        inverse = lax.rsqrt(total / hours + 1e-06)
        standard = (filtered[u].astype(F32) * inverse).astype(jnp.bfloat16)
        part[...] += jnp.dot(standard, omega[row, where, :], preferred_element_type=F32)

    own.wait()
    left.wait()
    right.wait()
    smooth(2, 0)
    pl.semaphore_wait(barrier, spaces + flat - 2)

    for part_of in range(2):
        for step in (1, -1):
            copies = halo(part_of, step)

            @pl.when((s < spaces - 1) if step > 0 else (s > 0))
            def _():
                for copy in copies:
                    copy.start()

    send_rims(0)
    send_rims(1)
    smooth(2, 1)
    load_omega.start()

    @pl.when(s == spaces - 1)
    def _():
        x[last : last + 2] = jnp.zeros((2, lon + 32, span), jnp.bfloat16)

    @pl.when(s == 0)
    def _():
        x[0:2] = jnp.zeros((2, lon + 32, span), jnp.bfloat16)

    @pl.when(t == 0)
    def _():
        series[:, :, 0:128] = jnp.zeros((rows, lon, 128), jnp.bfloat16)

    @pl.when(t == blocks - 1)
    def _():
        series[:, :, span + 128 : span + 256] = jnp.zeros((rows, lon, 128), jnp.bfloat16)

    part[...] = jnp.zeros(part.shape, F32)
    load_omega.wait()

    @pl.loop(2, units + LAG)
    def _(n):
        for part_of in range(2):

            @pl.when(n == 4 + 4 * part_of)
            def _():
                @pl.when(s < spaces - 1)
                def _():
                    halo_wait(part_of, -1, 1)

                @pl.when(s > 0)
                def _():
                    halo_wait(part_of, 1, 1)

        @pl.when((n == 4) | (n == 8))
        def _():
            @pl.loop(0, 2)
            def _(k):
                smooth(4 - 4 * k, (n - 4) // 4)

        @pl.when(n < units)
        def _():
            sent_rims(n - 2)
            send_rims(n)

        @pl.when(n < units + 2)
        def _():
            filter_unit(n - 2)

        @pl.when(n >= LAG)
        def _():
            sketch_unit(n - LAG)

    half = part.shape[1] // 2
    split = part[...].reshape(spaces, span // spaces, 2 * half)
    offered[...] = jnp.concatenate([split[:, :, :half], split[:, :, half:]], axis=1).astype(jnp.bfloat16)

    @pl.loop(1, spaces)
    def _(q):
        to, _ = across(q)
        pltpu.make_async_remote_copy(
            src_ref=offered.at[to],
            dst_ref=arrived.at[q - 1],
            send_sem=sum_sem.at[0],
            recv_sem=sum_sem.at[1],
            device_id=across(q),
            device_id_type=MESH,
        ).start()

    near = part[pl.ds(pl.multiple_of(s * 8, 8), 8), :]
    pltpu.make_async_copy(arrived, arrived, sum_sem.at[1]).wait()
    total = jnp.concatenate([near[:, :half], near[:, half:]], axis=0)
    for q in range(spaces - 1):
        total = total + arrived[q].astype(F32)
    own_ref[:, :half] = total[:8]
    own_ref[:, half:] = total[8:]
    mine_ref[...] = total.astype(jnp.bfloat16)
    pltpu.make_async_copy(mine_ref, all_ref.at[core, t, chip], gather_sem.at[t]).start()

    @pl.loop(1, flat)
    def _(e):
        pltpu.make_async_remote_copy(
            src_ref=mine_ref,
            dst_ref=all_ref.at[core, t, chip],
            send_sem=sent_sem,
            recv_sem=gather_sem.at[t],
            device_id=around(e),
            device_id_type=MESH,
        ).start()

    def pair(k):
        group = all_ref.at[core, lax.rem(t + blocks - k, blocks)]
        return pltpu.make_async_remote_copy(
            src_ref=group,
            dst_ref=group,
            send_sem=pair_sem.at[0, k],
            recv_sem=pair_sem.at[1, k],
            device_id=(2 * chip + 1 - core, t),
            device_id_type=MESH,
        )

    for k in range(blocks):
        sender = lax.rem(t + blocks - k, blocks)
        group = all_ref.at[core, sender]
        pltpu.make_async_copy(group, group, gather_sem.at[sender]).wait()
        pair(k).start()

    for part_of in range(2):
        for step in (1, -1):

            @pl.when((s < spaces - 1) if step > 0 else (s > 0))
            def _():
                halo_wait(part_of, step, 0)

    sent_rims(units - 2)
    sent_rims(units - 1)

    @pl.loop(0, units)
    def _(u):
        pltpu.make_async_copy(heard.at[u], heard.at[u], energy_sem.at[0, u]).wait()

    pltpu.make_async_copy(arrived, arrived, sum_sem.at[0]).wait()
    for k in range(blocks):
        whole = all_ref.at[core, k] if k else all_ref.at[core, k, pl.ds(0, chips - 1)]
        pltpu.make_async_copy(whole, whole, sent_sem).wait()
    for k in range(blocks):
        pair(k).wait()


def front(field, sketch, spaces, blocks):
    rows, lon, span = field.shape
    n = sketch.shape[2]
    piece, chips, units = 144, spaces // 2, 2 * rows
    vmem = pl.BlockSpec(memory_space=pltpu.VMEM)
    hbm = pl.BlockSpec(memory_space=pl.ANY)
    return pl.pallas_call(
        functools.partial(front_kernel, span * blocks),
        out_shape=(
            jax.ShapeDtypeStruct((2, blocks, chips, 16, n // 2), jnp.bfloat16),
            jax.ShapeDtypeStruct((8, n), F32),
        ),
        in_specs=[hbm, hbm, vmem, vmem],
        out_specs=(vmem, vmem),
        scratch_shapes=[
            pltpu.VMEM((rows + 4, lon + 32, span), jnp.bfloat16),
            pltpu.VMEM((rows, lon, span + 256), jnp.bfloat16),
            pltpu.VMEM((rows, lon, n), jnp.bfloat16),
            pltpu.VMEM((units, span, lon // 2), jnp.bfloat16),
            pltpu.VMEM((units, 1, lon // 2), F32),
            pltpu.VMEM((units, blocks - 1, 1, lon // 2), F32),
            pltpu.VMEM((span, n), F32),
            pltpu.VMEM((spaces, 16, n // 2), jnp.bfloat16),
            pltpu.VMEM((spaces - 1, 16, n // 2), jnp.bfloat16),
            pltpu.VMEM((16, n // 2), jnp.bfloat16),
            pltpu.SemaphoreType.DMA((3,)),
            pltpu.SemaphoreType.DMA,
            pltpu.SemaphoreType.DMA((2, 4)),
            pltpu.SemaphoreType.DMA((4, units)),
            pltpu.SemaphoreType.DMA((2, units)),
            pltpu.SemaphoreType.DMA((2,)),
            pltpu.SemaphoreType.DMA,
            pltpu.SemaphoreType.DMA((blocks,)),
            pltpu.SemaphoreType.DMA((2, blocks)),
        ],
        compiler_params=pltpu.CompilerParams(
            collective_id=0, has_side_effects=True, vmem_limit_bytes=56 * 2**20
        ),
        name="front",
    )(field, sketch, jnp.asarray(band_weights(span)), jnp.asarray(ring_weights(piece)))


def factor_block(m_ref):
    lane8 = lax.broadcasted_iota(jnp.int32, (8, 1), 0)
    for q in range(16):
        top = 8 * q
        p = m_ref[top:top + 8, :]
        cols = [jnp.broadcast_to(m_ref[top:128, top + k:top + k + 1], (128 - top, 128)) for k in range(8)]
        scaled = []
        for k in range(8):
            c = cols[k]
            d = c[k:k + 1, :]
            r = 1.0 / d
            for m in range(k + 1, 8):
                cols[m] = cols[m] - c * (cols[m][k:k + 1, :] * r)
            row = p[k:k + 1, :]
            t = row * jnp.concatenate([r, r], axis=1)
            below = jnp.where(lane8 > k, c[0:8, :], 0.0)
            p = p - jnp.concatenate([below, below], axis=1) * t
            scaled.append(t)
            s = lax.rsqrt(d)
            m_ref[top + k:top + k + 1, :] = row * jnp.concatenate([s, s], axis=1)
        if q < 15:
            left = m_ref[top + 8:128, 0:128]
            right = m_ref[top + 8:128, 128:256]
            for k in range(8):
                c = cols[k][8:, :]
                left = left - c * scaled[k][:, 0:128]
                right = right - c * scaled[k][:, 128:256]
            m_ref[top + 8:128, 0:128] = left
            m_ref[top + 8:128, 128:256] = right

def factor_kernel(root, y_ref, own_ref, basis_ref, r_ref, a_ref, m_ref, rest_ref):
    n = own_ref.shape[1]
    blocks = n // 128
    pairs = y_ref[...].astype(F32)
    y = jnp.concatenate([pairs[:, :8].reshape(-1, n // 2), pairs[:, 8:].reshape(-1, n // 2)], axis=1).astype(jnp.bfloat16)
    a_ref[...] = lax.dot_general(y, y, (((0,), (0,)), ((), ())), preferred_element_type=F32)
    rest_ref[...] = own_ref[...]
    row = lax.broadcasted_iota(jnp.int32, (128, 128), 0)
    col = lax.broadcasted_iota(jnp.int32, (128, 128), 1)

    @pl.loop(0, blocks)
    def _(b):
        here = pl.ds(pl.multiple_of(b * 128, 128), 128)
        m_ref[:, 0:128] = a_ref[here, here]
        m_ref[:, 128:256] = (row == col).astype(F32)
        factor_block(m_ref)
        inv = m_ref[:, 128:256]
        x = lax.dot_general(rest_ref[:, here], inv, (((1,), (1,)), ((), ())), precision=HI, preferred_element_type=F32)
        basis_ref[:, here] = x * root
        panel = jnp.dot(inv, a_ref[here, :], precision=HI, preferred_element_type=F32)
        wide = lax.broadcasted_iota(jnp.int32, (128, n), 1) >= (b + 1) * 128
        panel = jnp.where(wide, panel, 0.0)
        r_ref[here, :] = panel * (1.0 / root)
        r_ref[here, here] = jnp.where(row <= col, m_ref[:, 0:128], 0.0) * (1.0 / root)
        rest_ref[...] -= jnp.dot(x, panel, precision=HI, preferred_element_type=F32)
        a_ref[...] -= lax.dot_general(panel, panel, (((0,), (0,)), ((), ())), precision=HI, preferred_element_type=F32)

def factor(y, own, hours):
    n = own.shape[1]
    return pl.pallas_call(
        functools.partial(factor_kernel, math.sqrt(hours)),
        out_shape=(jax.ShapeDtypeStruct((own.shape[0], n), F32), jax.ShapeDtypeStruct((n, n), F32)),
        in_specs=[pl.BlockSpec(memory_space=pltpu.VMEM)] * 2,
        out_specs=(pl.BlockSpec(memory_space=pltpu.VMEM), pl.BlockSpec(memory_space=pltpu.VMEM)),
        scratch_shapes=[pltpu.VMEM((n, n), F32), pltpu.VMEM((128, 256), F32), pltpu.VMEM((own.shape[0], n), F32)],
        compiler_params=pltpu.CompilerParams(vmem_limit_bytes=32 * 2**20),
        name="factor",
    )(y, own)


def body(field, sketch):
    spaces, blocks = lax.axis_size("space"), lax.axis_size("tm")
    all_hours = field.shape[2] * blocks
    everyone, own = front(field, sketch, spaces, blocks)
    return factor(everyone.reshape(-1, 16, everyone.shape[4]), own, all_hours)


def solution(mesh):
    placed = (P("space", None, "tm"), P("space", None, None))
    return jax.shard_map(
        body, mesh=mesh, in_specs=placed, out_specs=(P(("tm", "space"), None), P()), check_vma=False
    )
```

time: 116 us -> 108 us (0.931)
  Pallas kernels: 113 us -> 105 us
    pallas_call x1, Pallas kernels: 93 us -> 84.9 us  [front(): pl.pallas_call(functools.partial(front_kernel, span * blocks), out_shape=...]
where the time goes in v4:
time: 108 us
  Pallas kernels  105 us (97%)
  local copies, waits for them, and re-layouts  1.93 us (2%)
    pallas_call x1, Pallas kernels, front(): pl.pallas_call(functools.partial(front_kernel, span * blocks), out_shape=...  84.9 us
    pallas_call x1, Pallas kernels, factor(): pl.pallas_call(functools.partial(factor_kernel, math.sqrt(hours)), out_sh...  20.3 us

profile of v4, /device:TPU:1, one launch (start us, length us, event | category | flops | bytes accessed | tf_op | source)
XLA Modules:
  0.0 107.8 jit_solution(12052753062724568465)
XLA Ops:
  0.6 84.9 %front.1 = (bf16[2,4,16,16,256]{4,3,2,1,0:T(8,128)(2,1)}, f32[8,512]{1,0:T(8,128)}) custom-call(bf16[6,1440,256]{2,1,0:T(8,128)(2,1)} %field_ref.1, bf16[6,1440,512]{2,1,0:T(8,128)(2,1)} %sketch_ref.1, bf16[256,512]{1,0:T(8,128)(2,1)} %constant.4.clone.band_ref, bf16[144,176]{1,0:T(8,128)(2,1)} %constant.5.clone.ring_ref), custom_call_target="tpu_custom_call" | custom-call | tf_op jit(solution)/shard_map/front/pallas_call | solution.py:389
  85.6 0.0 copy-start
  85.6 1.2 %copy-done = bf16[2,4,16,16,256]{4,3,2,1,0:T(8,128)(2,1)S(1)} copy-done((bf16[2,4,16,16,256]{4,3,2,1,0:T(8,128)(2,1)S(1)}, bf16[2,4,16,16,256]{4,3,2,1,0:T(8,128)(2,1)}, u32[]{:S(2)}) %copy-start) | copy-done | bytes 1048600
  86.8 0.0 copy-start.1
  86.8 0.7 copy-done.1
  87.5 20.3 %factor.1 = (f32[8,512]{1,0:T(8,128)}, f32[512,512]{1,0:T(8,128)}) custom-call(bf16[128,16,256]{2,1,0:T(8,128)(2,1)S(1)} %bitcast.1, f32[8,512]{1,0:T(8,128)S(1)} %copy-done.1), custom_call_target="tpu_custom_call" | custom-call | tf_op jit(solution)/shard_map/factor/pallas_call | solution.py:484
Async XLA Ops:
  85.6 1.2 %copy-start = (bf16[2,4,16,16,256]{4,3,2,1,0:T(8,128)(2,1)S(1)}, bf16[2,4,16,16,256]{4,3,2,1,0:T(8,128)(2,1)}, u32[]{:S(2)}) copy-start(bf16[2,4,16,16,256]{4,3,2,1,0:T(8,128)(2,1)} %get-tuple-element.4) | copy-start | bytes 3145732
  86.8 0.7 copy-start.1

commit v5 on v4

--- a/solution.py
+++ b/solution.py
@@ -11,7 +11,7 @@
 
 HALO = 120
 F32 = jnp.float32
-HI = lax.Precision.HIGHEST
+HI = lax.Precision.HIGH
 MESH = pl.DeviceIdType.MESH
 LAG = 4
 
@@ -54,6 +54,7 @@
     offered,
     arrived,
     mine_ref,
+    ready,
     load_sem,
     omega_sem,
     row_sem,
@@ -93,13 +94,16 @@
     right.start()
     load_omega = pltpu.make_async_copy(sketch_ref, omega, omega_sem)
 
-    @pl.loop(1, spaces)
-    def _(q):
-        pl.semaphore_signal(barrier, inc=1, device_id=across(q), device_id_type=MESH)
-
-    @pl.loop(1, flat)
-    def _(e):
-        pl.semaphore_signal(barrier, inc=1, device_id=around(e), device_id_type=MESH)
+    def tell(semaphore, radius):
+        for step in (radius, spaces - radius):
+            pl.semaphore_signal(semaphore, inc=1, device_id=across(step), device_id_type=MESH)
+
+    def tell_blocks(semaphore):
+        for q in range(1, blocks):
+            pl.semaphore_signal(semaphore, inc=1, device_id=(s, lax.rem(t + q, blocks)), device_id_type=MESH)
+
+    tell(barrier, 1)
+    tell_blocks(barrier)
 
     def halo(part_of, step):
         take = slice(rows - 2, rows) if step > 0 else slice(0, 2)
@@ -236,7 +240,7 @@
     left.wait()
     right.wait()
     smooth(2, 0)
-    pl.semaphore_wait(barrier, spaces + flat - 2)
+    pl.semaphore_wait(barrier, blocks + 1)
 
     for part_of in range(2):
         for step in (1, -1):
@@ -296,6 +300,17 @@
             sent_rims(n - 2)
             send_rims(n)
 
+        for k in range(5):
+
+            @pl.when(n == 5 + k)
+            def _():
+                if k:
+                    pl.semaphore_wait(ready.at[k - 1], 2)
+                if k < 4:
+                    tell(ready.at[k], 2**k)
+                else:
+                    tell_blocks(ready.at[k])
+
         @pl.when(n < units + 2)
         def _():
             filter_unit(n - 2)
@@ -304,6 +319,7 @@
         def _():
             sketch_unit(n - LAG)
 
+    pl.semaphore_wait(ready.at[4], blocks - 1)
     half = part.shape[1] // 2
     split = part[...].reshape(spaces, span // spaces, 2 * half)
     offered[...] = jnp.concatenate([split[:, :, :half], split[:, :, half:]], axis=1).astype(jnp.bfloat16)
@@ -405,6 +421,7 @@
             pltpu.VMEM((spaces, 16, n // 2), jnp.bfloat16),
             pltpu.VMEM((spaces - 1, 16, n // 2), jnp.bfloat16),
             pltpu.VMEM((16, n // 2), jnp.bfloat16),
+            pltpu.SemaphoreType.REGULAR((5,)),
             pltpu.SemaphoreType.DMA((3,)),
             pltpu.SemaphoreType.DMA,
             pltpu.SemaphoreType.DMA((2, 4)),

time: 108 us -> 104 us (0.963)
  Pallas kernels: 105 us -> 101 us
    pallas_call x1, Pallas kernels: 20.3 us -> 18 us  [factor(): pl.pallas_call(functools.partial(factor_kernel, math.sqrt(hours)), out_sh...]
    pallas_call x1, Pallas kernels: 84.9 us -> 83.4 us  [front(): pl.pallas_call(functools.partial(front_kernel, span * blocks), out_shape=...]
where the time goes in v5:
time: 104 us
  Pallas kernels  101 us (97%)
  local copies, waits for them, and re-layouts  1.93 us (2%)
    pallas_call x1, Pallas kernels, front(): pl.pallas_call(functools.partial(front_kernel, span * blocks), out_shape=...  83.4 us
    pallas_call x1, Pallas kernels, factor(): pl.pallas_call(functools.partial(factor_kernel, math.sqrt(hours)), out_sh...  18 us

profile of v5, /device:TPU:1, one launch (start us, length us, event | category | flops | bytes accessed | tf_op | source)
XLA Modules:
  0.0 104.0 jit_solution(340260383764169927)
XLA Ops:
  0.6 83.4 %front.1 = (bf16[2,4,16,16,256]{4,3,2,1,0:T(8,128)(2,1)}, f32[8,512]{1,0:T(8,128)}) custom-call(bf16[6,1440,256]{2,1,0:T(8,128)(2,1)} %field_ref.1, bf16[6,1440,512]{2,1,0:T(8,128)(2,1)} %sketch_ref.1, bf16[256,512]{1,0:T(8,128)(2,1)} %constant.4.clone.band_ref, bf16[144,176]{1,0:T(8,128)(2,1)} %constant.5.clone.ring_ref), custom_call_target="tpu_custom_call" | custom-call | tf_op jit(solution)/shard_map/front/pallas_call | solution.py:405
  84.0 0.0 copy-start
  84.0 1.2 %copy-done = bf16[2,4,16,16,256]{4,3,2,1,0:T(8,128)(2,1)S(1)} copy-done((bf16[2,4,16,16,256]{4,3,2,1,0:T(8,128)(2,1)S(1)}, bf16[2,4,16,16,256]{4,3,2,1,0:T(8,128)(2,1)}, u32[]{:S(2)}) %copy-start) | copy-done | bytes 1048600
  85.2 0.0 copy-start.1
  85.3 0.7 copy-done.1
  86.0 18.0 %factor.1 = (f32[8,512]{1,0:T(8,128)}, f32[512,512]{1,0:T(8,128)}) custom-call(bf16[128,16,256]{2,1,0:T(8,128)(2,1)S(1)} %bitcast.1, f32[8,512]{1,0:T(8,128)S(1)} %copy-done.1), custom_call_target="tpu_custom_call" | custom-call | tf_op jit(solution)/shard_map/factor/pallas_call | solution.py:501
Async XLA Ops:
  84.0 1.2 %copy-start = (bf16[2,4,16,16,256]{4,3,2,1,0:T(8,128)(2,1)S(1)}, bf16[2,4,16,16,256]{4,3,2,1,0:T(8,128)(2,1)}, u32[]{:S(2)}) copy-start(bf16[2,4,16,16,256]{4,3,2,1,0:T(8,128)(2,1)} %get-tuple-element.4) | copy-start | bytes 3145732
  85.2 0.7 copy-start.1

commit v6 on v5

--- a/solution.py
+++ b/solution.py
@@ -46,6 +46,7 @@
     own_ref,
     x,
     series,
+    packed,
     omega,
     filtered,
     energy,
@@ -74,15 +75,9 @@
     last = rows + 2
     chips = spaces // 2
     core, chip = lax.rem(s, 2), s // 2
-    flat = chips * blocks
-    mine = t * chips + chip
 
     def across(q):
         return lax.rem(s + q, spaces), t
-
-    def around(e):
-        to = lax.rem(mine + e, flat)
-        return 2 * lax.rem(to, chips) + core, to // chips
 
     barrier = pltpu.get_barrier_semaphore()
 
@@ -156,19 +151,51 @@
         row = jnp.where(early, 2 + lax.rem(u, 2), lax.rem(u, 4) + 4 - 6 * (lax.rem(u, 4) // 2))
         return row, pl.ds(pl.multiple_of(half * reach, 16), reach)
 
+    keep = packed.shape[2]
+    extra = reach - keep
+    pieces = HALO // 8
+    lane = lax.broadcasted_iota(jnp.int32, (extra, 128), 1)
+
+    def within(where, start, size):
+        return pl.ds(pl.multiple_of(where.start + start, 16), size)
+
+    def pack(u):
+        row, where = place(u)
+        for side, low, spare in ((0, span, lane < 8), (1, 128, lane >= HALO)):
+            tile = slice(low, low + 128)
+            ending = series[row, within(where, keep, extra), tile].astype(F32)
+            for k in range(pieces):
+                at = k * extra
+                same = series[row, within(where, at, extra), tile].astype(F32)
+                moved = pltpu.roll(ending, HALO - 8 * k, 1)
+                packed[side, lax.rem(u, 2), at : at + extra, :] = jnp.where(spare, moved, same).astype(jnp.bfloat16)
+            at = pieces * extra
+            packed[side, lax.rem(u, 2), at:keep, :] = series[row, within(where, at, keep - at), tile]
+
+    def unpack(u):
+        row, where = place(u)
+        for low, first in ((0, 8), (span + 128, 0)):
+            tile = slice(low, low + 128)
+            ending = jnp.zeros((extra, 128), F32)
+            for k in range(pieces):
+                moved = pltpu.roll(series[row, within(where, k * extra, extra), tile].astype(F32), 8 + 8 * k, 1)
+                at = first + 8 * k
+                ending = jnp.where((lane >= at) & (lane < at + 8), moved, ending)
+            series[row, within(where, keep, extra), tile] = ending.astype(jnp.bfloat16)
+
     def rims(u):
         row, where = place(u)
         before = pltpu.make_async_remote_copy(
-            src_ref=series.at[row, where, span : span + 128],
-            dst_ref=series.at[row, where, 0:128],
+            src_ref=packed.at[0, lax.rem(u, 2)],
+            dst_ref=series.at[row, within(where, 0, keep), 0:128],
             send_sem=rim_sem.at[0, u],
             recv_sem=rim_sem.at[1, u],
             device_id=(s, t + 1),
             device_id_type=MESH,
         )
         after = pltpu.make_async_remote_copy(
-            src_ref=series.at[row, where, 128:256],
-            dst_ref=series.at[row, where, span + 128 : span + 256],
+            src_ref=packed.at[1, lax.rem(u, 2)],
+            dst_ref=series.at[row, within(where, 0, keep), span + 128 : span + 256],
             send_sem=rim_sem.at[2, u],
             recv_sem=rim_sem.at[3, u],
             device_id=(s, t - 1),
@@ -177,6 +204,7 @@
         return before, after
 
     def send_rims(u):
+        pack(u)
         before, after = rims(u)
 
         @pl.when(t < blocks - 1)
@@ -210,6 +238,7 @@
         def _():
             after.wait_recv()
 
+        unpack(u)
         value = lax.dot_general(
             band_ref[...], series[row, where, :], (((1,), (1,)), ((), ())), preferred_element_type=F32
         ).astype(jnp.bfloat16)
@@ -251,8 +280,10 @@
                 for copy in copies:
                     copy.start()
 
-    send_rims(0)
-    send_rims(1)
+    @pl.loop(0, 2)
+    def _(u):
+        send_rims(u)
+
     smooth(2, 1)
     load_omega.start()
 
@@ -344,21 +375,55 @@
     own_ref[:, :half] = total[:8]
     own_ref[:, half:] = total[8:]
     mine_ref[...] = total.astype(jnp.bfloat16)
-    pltpu.make_async_copy(mine_ref, all_ref.at[core, t, chip], gather_sem.at[t]).start()
-
-    @pl.loop(1, flat)
-    def _(e):
+    all_ref[core, t, chip] = total.astype(jnp.bfloat16)
+    first, second = slice(0, half // 2), slice(half // 2, half)
+    near_chips = chips // 4
+
+    def block_peer(q):
+        return s, lax.rem(t + q, blocks)
+
+    def chip_peer(c):
+        return 2 * lax.rem(chip + c, chips) + core, t
+
+    def give(ref, to, kind, recv_sem, peer):
         pltpu.make_async_remote_copy(
-            src_ref=mine_ref,
-            dst_ref=all_ref.at[core, t, chip],
-            send_sem=sent_sem,
-            recv_sem=gather_sem.at[t],
-            device_id=around(e),
+            src_ref=ref,
+            dst_ref=to,
+            send_sem=sent_sem.at[kind],
+            recv_sem=recv_sem,
+            device_id=peer,
             device_id_type=MESH,
         ).start()
 
+    def settle(ref, semaphore):
+        pltpu.make_async_copy(ref, ref, semaphore).wait()
+
+    for q in range(1, blocks):
+        give(mine_ref.at[:, first], all_ref.at[core, t, chip, :, first], 0, gather_sem.at[0], block_peer(q))
+
+    @pl.loop(1, chips)
+    def _(c):
+        give(mine_ref.at[:, second], all_ref.at[core, t, chip, :, second], 1, gather_sem.at[1], chip_peer(c))
+
+    settle(all_ref.at[core, pl.ds(0, blocks - 1), chip, :, first], gather_sem.at[0])
+    column = all_ref.at[core, :, chip, :, first]
+
+    @pl.loop(1, chips)
+    def _(c):
+        give(column, column, 2, gather_sem.at[2 + chip // near_chips], chip_peer(c))
+
+    settle(all_ref.at[core, t, pl.ds(0, chips - 1), :, second], gather_sem.at[1])
+    plane = all_ref.at[core, t, :, :, second]
+    for q in range(1, blocks):
+        give(plane, plane, 3, gather_sem.at[5 + q], block_peer(q))
+
     def pair(k):
-        group = all_ref.at[core, lax.rem(t + blocks - k, blocks)]
+        j = k // 2
+        if k % 2:
+            group = all_ref.at[core, lax.rem(t + blocks - (0, 1, 3, 2)[j], blocks), :, :, second]
+        else:
+            at = lax.rem(chip // near_chips + j, 4) * near_chips
+            group = all_ref.at[core, :, pl.ds(at, near_chips), :, first]
         return pltpu.make_async_remote_copy(
             src_ref=group,
             dst_ref=group,
@@ -368,10 +433,17 @@
             device_id_type=MESH,
         )
 
-    for k in range(blocks):
-        sender = lax.rem(t + blocks - k, blocks)
-        group = all_ref.at[core, sender]
-        pltpu.make_async_copy(group, group, gather_sem.at[sender]).wait()
+    for k in (1, 0, 3, 2, 5, 4, 7, 6):
+        j = k // 2
+        if k % 2:
+            if j:
+                settle(plane, gather_sem.at[5 + (0, 1, 3, 2)[j]])
+        else:
+            count = near_chips - 1 if j == 0 else near_chips
+            settle(
+                all_ref.at[core, :, pl.ds(0, count), :, first],
+                gather_sem.at[2 + lax.rem(chip // near_chips + j, 4)],
+            )
         pair(k).start()
 
     for part_of in range(2):
@@ -389,10 +461,11 @@
         pltpu.make_async_copy(heard.at[u], heard.at[u], energy_sem.at[0, u]).wait()
 
     pltpu.make_async_copy(arrived, arrived, sum_sem.at[0]).wait()
-    for k in range(blocks):
-        whole = all_ref.at[core, k] if k else all_ref.at[core, k, pl.ds(0, chips - 1)]
-        pltpu.make_async_copy(whole, whole, sent_sem).wait()
-    for k in range(blocks):
+    settle(all_ref.at[core, pl.ds(0, blocks - 1), chip, :, first], sent_sem.at[0])
+    settle(all_ref.at[core, t, pl.ds(0, chips - 1), :, second], sent_sem.at[1])
+    settle(all_ref.at[core, :, pl.ds(0, chips - 1), :, first], sent_sem.at[2])
+    settle(all_ref.at[core, pl.ds(0, blocks - 1), :, :, second], sent_sem.at[3])
+    for k in range(8):
         pair(k).wait()
 
 
@@ -400,6 +473,7 @@
     rows, lon, span = field.shape
     n = sketch.shape[2]
     piece, chips, units = 144, spaces // 2, 2 * rows
+    keep = -(-lon * HALO // 4096) * 16
     vmem = pl.BlockSpec(memory_space=pltpu.VMEM)
     hbm = pl.BlockSpec(memory_space=pl.ANY)
     return pl.pallas_call(
@@ -413,6 +487,7 @@
         scratch_shapes=[
             pltpu.VMEM((rows + 4, lon + 32, span), jnp.bfloat16),
             pltpu.VMEM((rows, lon, span + 256), jnp.bfloat16),
+            pltpu.VMEM((2, 2, keep, 128), jnp.bfloat16),
             pltpu.VMEM((rows, lon, n), jnp.bfloat16),
             pltpu.VMEM((units, span, lon // 2), jnp.bfloat16),
             pltpu.VMEM((units, 1, lon // 2), F32),
@@ -428,9 +503,9 @@
             pltpu.SemaphoreType.DMA((4, units)),
             pltpu.SemaphoreType.DMA((2, units)),
             pltpu.SemaphoreType.DMA((2,)),
-            pltpu.SemaphoreType.DMA,
-            pltpu.SemaphoreType.DMA((blocks,)),
-            pltpu.SemaphoreType.DMA((2, blocks)),
+            pltpu.SemaphoreType.DMA((4,)),
+            pltpu.SemaphoreType.DMA((5 + blocks,)),
+            pltpu.SemaphoreType.DMA((2, 8)),
         ],
         compiler_params=pltpu.CompilerParams(
             collective_id=0, has_side_effects=True, vmem_limit_bytes=56 * 2**20

time: 104 us -> 102 us (0.981)
  Pallas kernels: 101 us -> 98.9 us
    pallas_call x1, Pallas kernels: 83.4 us -> 80.9 us  [front(): pl.pallas_call(functools.partial(front_kernel, span * blocks), out_shape=...]
where the time goes in v6:
time: 102 us
  Pallas kernels  98.9 us (97%)
  local copies, waits for them, and re-layouts  1.93 us (2%)
    pallas_call x1, Pallas kernels, front(): pl.pallas_call(functools.partial(front_kernel, span * blocks), out_shape=...  80.9 us
    pallas_call x1, Pallas kernels, factor(): pl.pallas_call(functools.partial(factor_kernel, math.sqrt(hours)), out_sh...  18 us

profile of v6, /device:TPU:1, one launch (start us, length us, event | category | flops | bytes accessed | tf_op | source)
XLA Modules:
  0.0 101.5 jit_solution(5761790435464320096)
XLA Ops:
  0.6 80.9 %front.1 = (bf16[2,4,16,16,256]{4,3,2,1,0:T(8,128)(2,1)}, f32[8,512]{1,0:T(8,128)}) custom-call(bf16[6,1440,256]{2,1,0:T(8,128)(2,1)} %field_ref.1, bf16[6,1440,512]{2,1,0:T(8,128)(2,1)} %sketch_ref.1, bf16[256,512]{1,0:T(8,128)(2,1)} %constant.4.clone.band_ref, bf16[144,176]{1,0:T(8,128)(2,1)} %constant.5.clone.ring_ref), custom_call_target="tpu_custom_call" | custom-call | tf_op jit(solution)/shard_map/front/pallas_call | solution.py:479
  81.6 0.0 copy-start
  81.6 1.2 %copy-done = bf16[2,4,16,16,256]{4,3,2,1,0:T(8,128)(2,1)S(1)} copy-done((bf16[2,4,16,16,256]{4,3,2,1,0:T(8,128)(2,1)S(1)}, bf16[2,4,16,16,256]{4,3,2,1,0:T(8,128)(2,1)}, u32[]{:S(2)}) %copy-start) | copy-done | bytes 1048600
  82.8 0.0 copy-start.1
  82.8 0.7 copy-done.1
  83.5 18.0 %factor.1 = (f32[8,512]{1,0:T(8,128)}, f32[512,512]{1,0:T(8,128)}) custom-call(bf16[128,16,256]{2,1,0:T(8,128)(2,1)S(1)} %bitcast.1, f32[8,512]{1,0:T(8,128)S(1)} %copy-done.1), custom_call_target="tpu_custom_call" | custom-call | tf_op jit(solution)/shard_map/factor/pallas_call | solution.py:576
Async XLA Ops:
  81.6 1.2 %copy-start = (bf16[2,4,16,16,256]{4,3,2,1,0:T(8,128)(2,1)S(1)}, bf16[2,4,16,16,256]{4,3,2,1,0:T(8,128)(2,1)}, u32[]{:S(2)}) copy-start(bf16[2,4,16,16,256]{4,3,2,1,0:T(8,128)(2,1)} %get-tuple-element.4) | copy-start | bytes 3145732
  82.8 0.7 copy-start.1

commit v7 on v6

--- a/solution.py
+++ b/solution.py
@@ -579,7 +579,7 @@
         in_specs=[pl.BlockSpec(memory_space=pltpu.VMEM)] * 2,
         out_specs=(pl.BlockSpec(memory_space=pltpu.VMEM), pl.BlockSpec(memory_space=pltpu.VMEM)),
         scratch_shapes=[pltpu.VMEM((n, n), F32), pltpu.VMEM((128, 256), F32), pltpu.VMEM((own.shape[0], n), F32)],
-        compiler_params=pltpu.CompilerParams(vmem_limit_bytes=32 * 2**20),
+        compiler_params=pltpu.CompilerParams(vmem_limit_bytes=62 * 2**20),
         name="factor",
     )(y, own)
 

time: 102 us -> 101 us (level)
  local copies, waits for them, and re-layouts: 1.93 us -> 0 us
  Pallas kernels: 98.9 us -> 100 us
    unnamed x4 -> x0, local copies, waits for them, and re-layouts: 1.93 us -> none
    pallas_call x1, Pallas kernels: 18 us -> 19.3 us  [factor(): pl.pallas_call(functools.partial(factor_kernel, math.sqrt(hours)), out_sh...]
where the time goes in v7:
time: 101 us
  Pallas kernels  100 us (99%)
    pallas_call x1, Pallas kernels, front(): pl.pallas_call(functools.partial(front_kernel, span * blocks), out_shape=...  80.9 us
    pallas_call x1, Pallas kernels, factor(): pl.pallas_call(functools.partial(factor_kernel, math.sqrt(hours)), out_sh...  19.3 us

profile of v7, /device:TPU:1, one launch (start us, length us, event | category | flops | bytes accessed | tf_op | source)
XLA Modules:
  0.0 100.8 jit_solution(10205170835609362314)
XLA Ops:
  0.6 80.9 %front.1 = (bf16[2,4,16,16,256]{4,3,2,1,0:T(8,128)(2,1)}, f32[8,512]{1,0:T(8,128)}) custom-call(bf16[6,1440,256]{2,1,0:T(8,128)(2,1)} %field_ref.1, bf16[6,1440,512]{2,1,0:T(8,128)(2,1)} %sketch_ref.1, bf16[256,512]{1,0:T(8,128)(2,1)} %constant.4.clone.band_ref, bf16[144,176]{1,0:T(8,128)(2,1)} %constant.5.clone.ring_ref), custom_call_target="tpu_custom_call" | custom-call | tf_op jit(solution)/shard_map/front/pallas_call | solution.py:479
  81.6 19.3 %factor.1 = (f32[8,512]{1,0:T(8,128)}, f32[512,512]{1,0:T(8,128)}) custom-call(bf16[128,16,256]{2,1,0:T(8,128)(2,1)} %bitcast.1, f32[8,512]{1,0:T(8,128)} %get-tuple-element.5.own_ref), custom_call_target="tpu_custom_call" | custom-call | tf_op jit(solution)/shard_map/factor/pallas_call | solution.py:576

commit v8 on v7

--- a/solution.py
+++ b/solution.py
@@ -13,7 +13,7 @@
 F32 = jnp.float32
 HI = lax.Precision.HIGH
 MESH = pl.DeviceIdType.MESH
-LAG = 4
+LAG = 5
 
 
 low_cutoff = 1.0 / 240.0

time: 101 us -> 101 us (level)
  no operation moved by 1% of the time
where the time goes in v8:
time: 101 us
  Pallas kernels  100 us (99%)
    pallas_call x1, Pallas kernels, front(): pl.pallas_call(functools.partial(front_kernel, span * blocks), out_shape=...  80.9 us
    pallas_call x1, Pallas kernels, factor(): pl.pallas_call(functools.partial(factor_kernel, math.sqrt(hours)), out_sh...  19.3 us

profile of v8, /device:TPU:1, one launch (start us, length us, event | category | flops | bytes accessed | tf_op | source)
XLA Modules:
  0.0 100.8 jit_solution(8829391748993804276)
XLA Ops:
  0.6 80.9 %front.1 = (bf16[2,4,16,16,256]{4,3,2,1,0:T(8,128)(2,1)}, f32[8,512]{1,0:T(8,128)}) custom-call(bf16[6,1440,256]{2,1,0:T(8,128)(2,1)} %field_ref.1, bf16[6,1440,512]{2,1,0:T(8,128)(2,1)} %sketch_ref.1, bf16[256,512]{1,0:T(8,128)(2,1)} %constant.4.clone.band_ref, bf16[144,176]{1,0:T(8,128)(2,1)} %constant.5.clone.ring_ref), custom_call_target="tpu_custom_call" | custom-call | tf_op jit(solution)/shard_map/front/pallas_call | solution.py:479
  81.6 19.3 %factor.1 = (f32[8,512]{1,0:T(8,128)}, f32[512,512]{1,0:T(8,128)}) custom-call(bf16[128,16,256]{2,1,0:T(8,128)(2,1)} %bitcast.1, f32[8,512]{1,0:T(8,128)} %get-tuple-element.5.own_ref), custom_call_target="tpu_custom_call" | custom-call | tf_op jit(solution)/shard_map/factor/pallas_call | solution.py:576
